TPU v7x, 32 devices: a whole 2x2x4 slice. The times are simulated.
32 devices in a mesh: section: 2 (over x), ctx: 16 (over z, y, core).
Axes of the slice: x: 2, y: 2, z: 4, core: 2. Of those that a mesh axis runs over, the one named last changes fastest.
Arguments:
- activations: bfloat16 [2, 24, 8192], P('section'), may hold values from -6 to 6
- act_frames: int32 [2, 24], replicated, may hold values from 0 to 191
- fresh_batch: bfloat16 [24, 8192], replicated, may hold values from -6 to 6
- fresh_frames: int32 [24], replicated, may hold values from 0 to 191
- norm_gain: float32 [2, 8192], P('section'), may hold values from 0.1 to 1.9
- cached_keys: bfloat16 [2, 12288, 1024], P('section', 'ctx'), may hold values from -64 to 64
- cached_values: bfloat16 [2, 12288, 1024], P('section', 'ctx'), may hold values from -6 to 6
- key_frames: int32 [12288], P('ctx'), may hold values from 0 to 191, never falling along the last dimension, each value on 1 to 128 neighbouring positions
Outputs:
- result: bfloat16 [2, 24, 8192], P('section')
Inputs may be any that keep to these rules, and one draw needn't show every extreme that they name: `key_frames`: frame indices never fall along the clip, and every frame of 0 to 191 holds at least one token.
All inputs are finite; a program needn't handle non-finite values.
Results may differ from a plain program's by a relative error of at most 0.019.
Values may be sent and summed in bfloat16 or wider, within the bound.
No kernel may reach another device: no remote copies, remote signals or barrier semaphores. Data moves between devices by JAX's collectives and lax.ppermute only.
A program may use at most 64 MiB of HBM per device.

v0:
```python
import functools
import math

import jax
import jax.numpy as jnp
from jax import lax
from jax.experimental import pallas as pl
from jax.experimental.pallas import tpu as pltpu
from jax.sharding import PartitionSpec as P

HEADS = 64
HD = 128
PAIR = 2
INNER = 2
BLOCKS = 4
STAT_ROWS = 16
HIDDEN = -(2.0**100)
SCALE = HD**-0.5 * math.log2(math.e)
MIB = 1 << 20

epsilon = 1e-05

WHOLE = pl.BlockSpec(memory_space=pltpu.VMEM)
IN_HBM = pl.BlockSpec(memory_space=pltpu.HBM)


def in_hbm(*arrays):
    return [pltpu.with_memory_space_constraint(a, pltpu.HBM) for a in arrays]


def in_vmem(*arrays):
    return [pltpu.with_memory_space_constraint(a, pltpu.VMEM) for a in arrays]


def place_here():
    return lax.axis_index("ctx") % PAIR


def inner_here():
    return lax.axis_index("ctx") // PAIR % INNER


def outer_here():
    return lax.axis_index("ctx") // (PAIR * INNER)


def in_first_section():
    return lax.axis_index("section") == 0


def swapped(block):
    return lax.ppermute(block, "ctx", [(i, i ^ 1) for i in range(lax.axis_size("ctx"))])


def from_inner(block):
    size = lax.axis_size("ctx")
    return lax.ppermute(block, "ctx", [(i, i ^ PAIR ^ 1) for i in range(size)])


def from_outer(blocks, other_place=1):
    size = lax.axis_size("ctx")
    got = [
        lax.ppermute(
            block, "ctx", [(i, i ^ (INNER * PAIR * d) ^ other_place) for i in range(size)]
        )
        for d, block in reversed(list(enumerate(blocks, 1)))
    ]
    return got[::-1]


def from_section_before(block, step):
    sections, size = lax.axis_size("section"), lax.axis_size("ctx")
    route = [
        (s * size + i, (s + 1) * size + (i ^ (PAIR * step) ^ 1))
        for s in range(sections - 1)
        for i in range(size)
    ]
    return lax.ppermute(block, ("section", "ctx"), route)


def head_rows(block):
    return jnp.concatenate(
        [block[:, at : at + HD] for at in range(0, block.shape[1], HD)], axis=0
    )


def row_of(ref):
    return jnp.concatenate([ref[i : i + 1] for i in range(ref.shape[0])], axis=1)


def columns_of(index, ref, width):
    return ref.at[:, pl.ds(pl.multiple_of(index * width, HD), width)]


def on_diagonal(rows):
    shape = (rows, HD)
    return lax.broadcasted_iota(jnp.int32, shape, 0) == lax.broadcasted_iota(jnp.int32, shape, 1)


def queries_of(x, gain):
    rows = head_rows(x.astype(jnp.float32))
    gain = head_rows(jnp.broadcast_to(gain, x.shape))
    norm = lax.rsqrt(jnp.mean(rows * rows, axis=-1, keepdims=True) + epsilon)
    return (rows * norm * gain).astype(jnp.bfloat16)


def bias_of(keys_ref, frames):
    length = keys_ref.shape[0] - STAT_ROWS
    width = keys_ref.shape[1]
    rows = -(-length // width)
    tail = keys_ref[length:].astype(jnp.float32)
    key_frames = jnp.concatenate([tail[i : i + 1] for i in range(rows)], axis=1)[:, :length]
    return jnp.where(key_frames <= frames, 0.0, HIDDEN)[None]


def scores(queries, key_block, bias):
    count, keys, tokens = queries.shape[0], key_block.shape[0], bias.shape[1]
    raw = lax.dot_general(
        queries, key_block, (((1,), (1,)), ((), ())), preferred_element_type=jnp.float32
    )
    raw = raw.reshape(count // tokens, tokens, keys) * SCALE + bias
    return raw.reshape(count, keys)


def top_of(raw):
    top = jnp.max(raw, axis=-1, keepdims=True)
    return top.astype(jnp.bfloat16).astype(jnp.float32)


def weigh(raw, top, value_block):
    probs = jnp.exp2(raw - top).astype(jnp.bfloat16)
    ones = jnp.ones((value_block.shape[0], HD), jnp.bfloat16)
    return jnp.dot(
        probs, jnp.concatenate([value_block, ones], axis=1), preferred_element_type=jnp.float32
    )


def groups_of(count):
    groups = -(-count // HD)
    held = count // groups
    return [slice(c * held, (c + 1) * held) for c in range(groups)]


def write_chunk(out_ref, weighted, tops, totals):
    count = weighted.shape[0]
    line = lax.broadcasted_iota(jnp.int32, (STAT_ROWS, HD), 0)
    stats = jnp.zeros((STAT_ROWS, HD), jnp.float32)
    for c, (top, total) in enumerate(zip(tops, totals)):
        high = total.astype(jnp.bfloat16).astype(jnp.float32)
        for n, row in enumerate((top, high, total - high)):
            stats = jnp.where(line == 3 * c + n, row, stats)
    out_ref[:count] = weighted.astype(jnp.bfloat16)
    out_ref[count:] = stats.astype(jnp.bfloat16)


def write_sums(out_ref, weighted, top, total):
    groups = groups_of(weighted.shape[0])
    diagonal = on_diagonal(groups[0].stop)

    def rows(column):
        column = jnp.broadcast_to(column, weighted.shape)
        return [
            jnp.sum(jnp.where(diagonal, column[group], 0.0), axis=0, keepdims=True)
            for group in groups
        ]

    write_chunk(out_ref, weighted, rows(top), rows(total))


def joined(parts, normed, x=None):
    count = parts[0].shape[0] - STAT_ROWS
    groups = groups_of(count)
    diagonal = on_diagonal(groups[0].stop)
    stats = [part[count:].astype(jnp.float32) for part in parts]
    values, tops, totals = [], [], []
    for c, group in enumerate(groups):
        points = [s[3 * c : 3 * c + 1] for s in stats]
        top = functools.reduce(jnp.maximum, points)
        factors = [jnp.exp2(point - top) for point in points]
        total = sum(
            f * (s[3 * c + 1 : 3 * c + 2] + s[3 * c + 2 : 3 * c + 3])
            for f, s in zip(factors, stats)
        )
        if normed:
            inverse = 1.0 / total
            factors = [f * inverse for f in factors]
        terms = list(zip(factors, parts)) + ([] if x is None else [(total, x)])
        value = 0.0
        for factor, part in terms:
            weight = jnp.where(diagonal, factor, 0.0)[:, : group.stop - group.start]
            high = weight.astype(jnp.bfloat16)
            low = (weight - high.astype(jnp.float32)).astype(jnp.bfloat16)
            for term in (high, low):
                value = value + jnp.dot(term, part[group], preferred_element_type=jnp.float32)
        values.append(value)
        tops.append(top)
        totals.append(total)
    return jnp.concatenate(values, axis=0), tops, totals


def halve(staged_ref, copies, own_ref, given_ref, gift_ref, gift_sems, tail):
    length, width = staged_ref.shape
    half, step = width // PAIR, length // BLOCKS
    if tail is not None:
        gift_ref[length:] = tail()
        own_ref[length:] = tail()
    place = place_here()
    gifts = []
    for b in range(BLOCKS):
        if copies:
            copies[b].wait()
        rows = pl.ds(b * step, step)
        gift_ref[rows] = columns_of(1 - place, staged_ref.at[rows], half)[...]
        own_ref[rows] = columns_of(place, staged_ref.at[rows], half)[...]
        if b == BLOCKS - 1:
            rows = pl.ds(b * step, gift_ref.shape[0] - b * step)
        gifts.append(pltpu.make_async_copy(gift_ref.at[rows], given_ref.at[rows], gift_sems.at[b]))
        gifts[-1].start()
    return gifts


def load_keys_kernel(
    key_frames_in, keys_in, own_ref, given_ref,
    key_frames_ref, staged_ref, gift_ref, sems, gift_sems, small_sem,
):
    length, half = staged_ref.shape[0], own_ref.shape[1]
    small = pltpu.make_async_copy(key_frames_in, key_frames_ref, small_sem)
    small.start()

    def tail():
        row = row_of(key_frames_ref).astype(jnp.float32)
        lines = -(-length // half)
        row = jnp.concatenate([row, jnp.zeros((1, lines * half - length), jnp.float32)], axis=1)
        line = lax.broadcasted_iota(jnp.int32, (STAT_ROWS, half), 0)
        lower = jnp.zeros((STAT_ROWS, half), jnp.float32)
        for n in range(lines):
            lower = jnp.where(line == n, row[:, n * half : (n + 1) * half], lower)
        return lower.astype(jnp.bfloat16)

    copies, step = [], length // BLOCKS
    for b in range(BLOCKS):
        rows = pl.ds(b * step, step)
        copies.append(pltpu.make_async_copy(keys_in.at[rows], staged_ref.at[rows], sems.at[b]))
        copies[-1].start()
    small.wait()
    for gift in halve(staged_ref, copies, own_ref, given_ref, gift_ref, gift_sems, tail):
        gift.wait()


def load_keys(key_frames, keys):
    length, width = keys.shape
    shape = (length + STAT_ROWS, width // PAIR)
    return pl.pallas_call(
        load_keys_kernel,
        in_specs=[IN_HBM] * 2,
        out_specs=[WHOLE, IN_HBM],
        out_shape=[pltpu.VMEM(shape, keys.dtype), pltpu.HBM(shape, keys.dtype)],
        scratch_shapes=[
            pltpu.VMEM(key_frames.shape, key_frames.dtype),
            pltpu.VMEM((length, width), keys.dtype),
            pltpu.VMEM(shape, keys.dtype),
            pltpu.SemaphoreType.DMA((BLOCKS,)),
            pltpu.SemaphoreType.DMA((BLOCKS,)),
            pltpu.SemaphoreType.DMA,
        ],
        cost_estimate=pl.CostEstimate(
            flops=0, bytes_accessed=2 * length * width, transcendentals=0
        ),
        compiler_params=pltpu.CompilerParams(vmem_limit_bytes=16 * MIB),
        name="load_keys",
    )(*in_hbm(key_frames, keys))


def load_values_kernel(
    values_ref, act_frames_in, fresh_frames_in, batch_in, fresh_in, gain_in,
    own_ref, given_ref, batches_ref, gain_ref, frames_ref,
    act_frames_ref, fresh_frames_ref, gift_ref, gift_sems, small_sems,
):
    place, half = place_here(), gain_ref.shape[1]
    small = [
        (act_frames_in, act_frames_ref),
        (fresh_frames_in, fresh_frames_ref),
        (columns_of(place, batch_in, half), batches_ref.at[0]),
        (columns_of(place, gain_in, half), gain_ref),
        (columns_of(place, fresh_in, half), batches_ref.at[1]),
    ]
    small = [pltpu.make_async_copy(a, b, small_sems.at[n]) for n, (a, b) in enumerate(small)]
    for copy in small:
        copy.start()
    gifts = halve(values_ref, [], own_ref, given_ref, gift_ref, gift_sems, None)
    for copy in small[:2]:
        copy.wait()

    tokens = frames_ref.shape[1]
    section = lax.axis_index("section")
    own_row = act_frames_ref[pl.ds(section, 1), :].astype(jnp.float32)
    prior_row = act_frames_ref[pl.ds(jnp.maximum(section - 1, 0), 1), :].astype(jnp.float32)
    fresh_row = fresh_frames_ref[...].astype(jnp.float32)
    next_row = jnp.where(in_first_section(), fresh_row, prior_row)
    shape = (tokens, tokens)
    diagonal = lax.broadcasted_iota(jnp.int32, shape, 0) == lax.broadcasted_iota(jnp.int32, shape, 1)
    for tick, row in enumerate((own_row, next_row)):
        column = jnp.sum(jnp.where(diagonal, row, 0.0), axis=1, keepdims=True)
        frames_ref[tick] = jnp.broadcast_to(column, (tokens, HD))

    for copy in small[2:] + gifts:
        copy.wait()


def load_values(act_frames, fresh_frames, values, batch, fresh, gain):
    length, width = values.shape
    tokens, model = batch.shape
    half = model // PAIR
    shape = (length, width // PAIR)
    return pl.pallas_call(
        load_values_kernel,
        in_specs=[WHOLE] + [IN_HBM] * 5,
        out_specs=[WHOLE, IN_HBM] + [WHOLE] * 3,
        out_shape=[
            pltpu.VMEM(shape, values.dtype),
            pltpu.HBM(shape, values.dtype),
            pltpu.VMEM((2, tokens, half), batch.dtype),
            pltpu.VMEM((1, half), gain.dtype),
            pltpu.VMEM((2, tokens, HD), jnp.float32),
        ],
        scratch_shapes=[
            pltpu.VMEM(act_frames.shape, act_frames.dtype),
            pltpu.VMEM(fresh_frames.shape, fresh_frames.dtype),
            pltpu.VMEM(shape, values.dtype),
            pltpu.SemaphoreType.DMA((BLOCKS,)),
            pltpu.SemaphoreType.DMA((5,)),
        ],
        cost_estimate=pl.CostEstimate(
            flops=0, bytes_accessed=2 * length * width, transcendentals=0
        ),
        compiler_params=pltpu.CompilerParams(vmem_limit_bytes=16 * MIB),
        name="load_values",
    )(*in_vmem(values), *in_hbm(act_frames, fresh_frames, batch, fresh, gain))


def begin_kernel(
    gain_ref, frames_ref, batches_ref, keys_ref, values_ref,
    queries_ref, sums_ref, stats_ref, share_ref,
):
    length = values_ref.shape[0]
    kv_here = values_ref.shape[1] // HD
    count, width = queries_ref.shape[0] // kv_here, gain_ref.shape[1] // kv_here
    bias = bias_of(keys_ref, frames_ref[0, :, :1])
    share_ref[...] = columns_of(outer_here(), batches_ref.at[0], share_ref.shape[1])[...]
    for g in range(kv_here):
        rows, columns = slice(g * count, (g + 1) * count), slice(g * width, (g + 1) * width)
        block = slice(g * HD, (g + 1) * HD)
        queries = queries_of(batches_ref[0, :, columns], gain_ref[:, columns])
        queries_ref[rows] = queries
        raw = scores(queries, keys_ref[:length, block], bias)
        top = top_of(raw)
        both = weigh(raw, top, values_ref[:, block])
        sums_ref[rows] = both[:, :HD]
        lane = lax.broadcasted_iota(jnp.int32, (count, HD), 1)
        stats_ref[rows] = jnp.where(lane < HD // 2, top, both[:, HD:])


def begin(gain, frames, batches, keys, values):
    length, width = values.shape
    _, tokens, half = batches.shape
    queries = HEADS // PAIR * tokens
    return pl.pallas_call(
        begin_kernel,
        in_specs=[WHOLE] * 5,
        out_specs=[WHOLE] * 4,
        out_shape=[
            jax.ShapeDtypeStruct((queries, HD), jnp.bfloat16),
            jax.ShapeDtypeStruct((queries, HD), jnp.float32),
            jax.ShapeDtypeStruct((queries, HD), jnp.float32),
            jax.ShapeDtypeStruct((tokens, half * HD // width), batches.dtype),
        ],
        cost_estimate=pl.CostEstimate(
            flops=2 * queries * length * 3 * HD,
            bytes_accessed=4 * length * width,
            transcendentals=queries * length,
        ),
        compiler_params=pltpu.CompilerParams(vmem_limit_bytes=16 * MIB),
        name="begin",
    )(*in_vmem(gain, frames, batches, keys, values))


def finish_kernel(
    d, kv_here, frames_ref, queries_ref, sums_ref, stats_ref, keys_ref, values_ref, out_ref
):
    length, count = values_ref.shape[0], queries_ref.shape[0] // kv_here
    g = outer_here() ^ d
    bias = bias_of(keys_ref, frames_ref[0, :, :1])
    rows = pl.ds(pl.multiple_of(g * count, count), count)
    raw = scores(queries_ref[rows], columns_of(g, keys_ref.at[:length], HD)[...], bias)
    stats = stats_ref[rows]
    before, totals = stats[:, :1], stats[:, HD // 2 : HD // 2 + 1]
    top = jnp.maximum(before, top_of(raw))
    factor = jnp.exp2(before - top)
    both = weigh(raw, top, columns_of(g, values_ref, HD)[...])
    weighted = both[:, :HD] + sums_ref[rows] * factor
    write_sums(out_ref, weighted, top, both[:, HD:] + totals * factor)


def chunk_call(kernel, name, d, kv_here, count, length, operands):
    return pl.pallas_call(
        functools.partial(kernel, d, kv_here),
        in_specs=[WHOLE] * len(operands),
        out_specs=WHOLE,
        out_shape=jax.ShapeDtypeStruct((count + STAT_ROWS, HD), jnp.bfloat16),
        cost_estimate=pl.CostEstimate(
            flops=2 * count * length * 3 * HD,
            bytes_accessed=4 * length * HD,
            transcendentals=count * length,
        ),
        compiler_params=pltpu.CompilerParams(vmem_limit_bytes=16 * MIB),
        name=name,
    )(*in_vmem(*operands))


def finish(d, frames, queries, sums, stats, keys, values):
    length, width = values.shape
    kv_here = width // HD
    operands = (frames, queries, sums, stats, keys, values)
    count = queries.shape[0] // kv_here
    return chunk_call(finish_kernel, "finish", d, kv_here, count, length, operands)


def partials_kernel(d, kv_here, gain_ref, frames_ref, batches_ref, *refs):
    kv_refs, (handed_ref, out_ref) = (refs[0:2], refs[2:4]), refs[4:]
    length, width = kv_refs[0][1].shape[0], handed_ref.shape[1]
    g = outer_here() ^ d
    fresh = columns_of(g, batches_ref.at[1], width)[...].astype(jnp.float32)
    x = jnp.where(in_first_section(), fresh, handed_ref[...].astype(jnp.float32))
    queries = queries_of(x, columns_of(g, gain_ref, width)[...])
    raws = [
        scores(
            queries,
            columns_of(g, keys_ref.at[:length], HD)[...],
            bias_of(keys_ref, frames_ref[1, :, :1]),
        )
        for keys_ref, _ in kv_refs
    ]
    top = functools.reduce(jnp.maximum, [top_of(raw) for raw in raws])
    both = sum(
        weigh(raw, top, columns_of(g, values_ref, HD)[...])
        for raw, (_, values_ref) in zip(raws, kv_refs)
    )
    write_sums(out_ref, both[:, :HD], top, both[:, HD:])


def partials(d, gain, frames, batches, own, got, handed):
    length, width = own[1].shape
    tokens = batches.shape[1]
    count = handed.shape[1] // HD * tokens
    operands = (gain, frames, batches, *own, *got, handed)
    return chunk_call(
        partials_kernel, "partials", d, width // HD, count, PAIR * length, operands
    )


def merge_kernel(*refs):
    *parts, out_ref = refs
    write_chunk(out_ref, *joined(parts, False))


def merge_first_kernel(*refs):
    *parts, share_ref, out_ref = refs
    x = head_rows(share_ref[...].astype(jnp.float32)).astype(jnp.bfloat16)
    write_chunk(out_ref, *joined(parts, False, x))


def merge(kernel, *parts):
    return pl.pallas_call(
        kernel,
        in_specs=[WHOLE] * len(parts),
        out_specs=WHOLE,
        out_shape=jax.ShapeDtypeStruct(parts[0].shape, parts[0].dtype),
        compiler_params=pltpu.CompilerParams(vmem_limit_bytes=8 * MIB),
        name="merge",
    )(*in_vmem(*parts))


def combined(one_ref, two_ref, x, out_ref):
    one, two = one_ref[...].astype(jnp.float32), two_ref[...].astype(jnp.float32)
    here = inner_here() == 0
    parts = [jnp.where(here, one, two), jnp.where(here, two, one)]
    total, _, _ = joined([part.astype(jnp.bfloat16) for part in parts], True)
    if x is not None:
        total = head_rows(x) + total
    tokens = out_ref.shape[0]
    for h in range(total.shape[0] // tokens):
        piece = total[h * tokens : (h + 1) * tokens]
        out_ref[:, h * HD : (h + 1) * HD] = piece.astype(jnp.bfloat16)


def combine_kernel(one_ref, two_ref, out_ref):
    combined(one_ref, two_ref, None, out_ref)


def combine_last_kernel(one_ref, two_ref, batches_ref, handed_ref, out_ref):
    fresh = columns_of(outer_here(), batches_ref.at[1], out_ref.shape[1])[...]
    x = jnp.where(
        in_first_section(), fresh.astype(jnp.float32), handed_ref[...].astype(jnp.float32)
    )
    combined(one_ref, two_ref, x, out_ref)


def combine(kernel, tokens, one, two, *rest):
    width = (one.shape[0] - STAT_ROWS) // tokens * HD
    return pl.pallas_call(
        kernel,
        in_specs=[WHOLE] * (2 + len(rest)),
        out_specs=WHOLE,
        out_shape=jax.ShapeDtypeStruct((tokens, width), jnp.bfloat16),
        compiler_params=pltpu.CompilerParams(vmem_limit_bytes=8 * MIB),
        name="combine",
    )(*in_vmem(one, two, *rest))


def assemble_kernel(*refs):
    *pieces, out_ref = refs
    outers, width = len(pieces) // PAIR, pieces[0].shape[1]
    for n, refs in enumerate((pieces[:outers], pieces[outers:])):
        place = (place_here() + n) % PAIR
        for d, ref in enumerate(refs):
            columns_of(place * outers + (outer_here() ^ d), out_ref, width)[...] = ref[...]


def assemble(mine, others):
    tokens, width = mine[0].shape
    pieces = [*mine, *others]
    return pl.pallas_call(
        assemble_kernel,
        in_specs=[WHOLE] * len(pieces),
        out_specs=WHOLE,
        out_shape=jax.ShapeDtypeStruct((tokens, len(pieces) * width), jnp.bfloat16),
        compiler_params=pltpu.CompilerParams(vmem_limit_bytes=8 * MIB),
        name="assemble",
    )(*in_vmem(*pieces))


def body(
    activations,
    act_frames,
    fresh_batch,
    fresh_frames,
    norm_gain,
    cached_keys,
    cached_values,
    key_frames,
):
    own_keys, given_keys = load_keys(key_frames.reshape(-1, HD), cached_keys[0])
    got_keys = swapped(given_keys)
    own_values, given_values, batches, gain, frames = load_values(
        act_frames, fresh_frames[None], cached_values[0], activations[0], fresh_batch, norm_gain
    )
    got_values = swapped(given_values)
    own, got = (own_keys, own_values), (got_keys, got_values)

    tokens = fresh_batch.shape[0]
    outers = lax.axis_size("ctx") // (INNER * PAIR)
    *terms, share = begin(gain, frames, batches, *own)
    chunk, *others = [finish(d, frames, *terms, *got) for d in range(outers)]
    chunk = merge(merge_first_kernel, *from_outer(others, 0)[::-1], chunk, share)
    one, two = [from_section_before(chunk, step) for step in range(INNER)]
    handed = combine(combine_kernel, tokens, one, two)
    handed = [swapped(handed), *from_outer([handed] * len(others))]

    chunk, *others = [
        partials(d, gain, frames, batches, own, got, piece) for d, piece in enumerate(handed)
    ]
    chunk = merge(merge_kernel, *from_outer(others)[::-1], swapped(chunk))
    one, two = swapped(chunk), from_inner(chunk)
    share = combine(combine_last_kernel, tokens, one, two, batches, handed[0])
    theirs = [swapped(share), *from_outer([share] * len(others))]
    return assemble([share, *(swapped(piece) for piece in theirs[1:])], theirs)[None]


def solution(mesh):
    placed = (
        P("section", None, None),
        P(),
        P(),
        P(),
        P("section", None),
        P("section", "ctx", None),
        P("section", "ctx", None),
        P("ctx"),
    )
    return jax.shard_map(
        body, mesh=mesh, in_specs=placed, out_specs=P("section", None, None), check_vma=False
    )
```

profile of v0, /device:TPU:0, one launch (start us, length us, event | category | flops | bytes accessed | tf_op | source)
XLA Modules:
  0.0 56.9 jit_solution(5268380252074164125)
XLA Ops:
  0.0 2.3 %load_keys.1 = (bf16[784,512]{1,0:T(8,128)(2,1)S(1)}, bf16[784,512]{1,0:T(8,128)(2,1)}) custom-call(s32[6,128]{1,0:T(8,128)} %bitcast.9, bf16[768,1024]{1,0:T(8,128)(2,1)} %bitcast.7), custom_call_target="tpu_custom_call" | custom-call | bytes 1572864 | tf_op jit(solution)/shard_map/load_keys/pallas_call | solution.py:253
  2.3 0.5 collective-permute-start
  2.8 1.4 %load_values.1 = (bf16[768,512]{1,0:T(8,128)(2,1)S(1)}, bf16[768,512]{1,0:T(8,128)(2,1)}, bf16[2,24,4096]{2,1,0:T(8,128)(2,1)S(1)}, f32[1,4096]{1,0:T(1,128)S(1)}, f32[2,24,128]{2,1,0:T(8,128)S(1)}) custom-call(bf16[768,1024]{1,0:T(8,128)(2,1)S(1)} %bitcast.6, s32[2,24]{1,0:T(2,128)} %act_frames_in.1, s32[1,24]{1,0:T(1,128)} %bitcast.10, ...), custom_call_target="tpu_custom_call" | custom-call | bytes 1572864 | tf_op jit(solution)/shard_map/load_values/pallas_call | solution.py:315
  4.3 0.1 collective-permute-start.1
  4.4 1.3 %begin.1 = (bf16[768,128]{1,0:T(8,128)(2,1)S(1)}, f32[768,128]{1,0:T(8,128)S(1)}, f32[768,128]{1,0:T(8,128)S(1)}, bf16[24,1024]{1,0:T(8,128)(2,1)S(1)}) custom-call(f32[1,4096]{1,0:T(1,128)S(1)} %get-tuple-element.16.gain_ref, f32[2,24,128]{2,1,0:T(8,128)S(1)} %get-tuple-element.17.frames_ref, bf16[2,24,4096]{2,1,0:T(8,128)(2,1)S(1)} %get-tuple-element.18.batches_ref, ...), custom_call_target="tpu_custom_call" | custom-call | flops 452984832 | bytes 1572864 | tf_op jit(solution)/shard_map/begin/pallas_call | solution.py:367
  5.7 1.1 %collective-permute-done.1.values_ref.refs_3_ = bf16[768,512]{1,0:T(8,128)(2,1)S(1)} collective-permute-done((bf16[768,512]{1,0:T(8,128)(2,1)}, bf16[768,512]{1,0:T(8,128)(2,1)S(1)}, u32[]{:S(2)}, u32[]{:S(2)}) %collective-permute-start.1) | collective-permute-done | bytes 786464 | tf_op jit(solution)/shard_map/ppermute | solution.py:52
  6.8 0.8 %finish.4 = bf16[208,128]{1,0:T(8,128)(2,1)S(1)} custom-call(f32[2,24,128]{2,1,0:T(8,128)S(1)} %get-tuple-element.17.frames_ref, bf16[768,128]{1,0:T(8,128)(2,1)S(1)} %get-tuple-element.23.queries_ref, f32[768,128]{1,0:T(8,128)S(1)} %get-tuple-element.24.sums_ref, f32[768,128]{1,0:T(8,128)S(1)} %get-tuple-element.25.stats_ref, ...), custom_call_target="tpu_custom_call" | custom-call | flops 113246208 | bytes 393216 | tf_op jit(solution)/shard_map/finish/pallas_call | solution.py:405
  7.6 4.8 %collective-permute-start.2 = (bf16[208,128]{1,0:T(8,128)(2,1)S(1)}, bf16[208,128]{1,0:T(8,128)(2,1)S(1)}, u32[]{:S(2)}, u32[]{:S(2)}) collective-permute-start(bf16[208,128]{1,0:T(8,128)(2,1)S(1)} %finish.4), channel_id=1, source_target_pairs={{0,12},{1,13},{2,14},{3,15},{4,8},{5,9},{6,10},{7,11},{8,4},{9,5},... | collective-permute-start | bytes 159752 | tf_op jit(solution)/shard_map/ppermute | solution.py:63
  12.4 0.7 %finish.5 = bf16[208,128]{1,0:T(8,128)(2,1)S(1)} custom-call(f32[2,24,128]{2,1,0:T(8,128)S(1)} %get-tuple-element.17.frames_ref, bf16[768,128]{1,0:T(8,128)(2,1)S(1)} %get-tuple-element.23.queries_ref, f32[768,128]{1,0:T(8,128)S(1)} %get-tuple-element.24.sums_ref, f32[768,128]{1,0:T(8,128)S(1)} %get-tuple-element.25.stats_ref, ...), custom_call_target="tpu_custom_call" | custom-call | flops 113246208 | bytes 393216 | tf_op jit(solution)/shard_map/finish/pallas_call | solution.py:405
  13.2 0.8 %finish.6 = bf16[208,128]{1,0:T(8,128)(2,1)S(1)} custom-call(f32[2,24,128]{2,1,0:T(8,128)S(1)} %get-tuple-element.17.frames_ref, bf16[768,128]{1,0:T(8,128)(2,1)S(1)} %get-tuple-element.23.queries_ref, f32[768,128]{1,0:T(8,128)S(1)} %get-tuple-element.24.sums_ref, f32[768,128]{1,0:T(8,128)S(1)} %get-tuple-element.25.stats_ref, ...), custom_call_target="tpu_custom_call" | custom-call | flops 113246208 | bytes 393216 | tf_op jit(solution)/shard_map/finish/pallas_call | solution.py:405
  14.0 0.6 %collective-permute-start.4 = (bf16[208,128]{1,0:T(8,128)(2,1)S(1)}, bf16[208,128]{1,0:T(8,128)(2,1)S(1)}, u32[]{:S(2)}, u32[]{:S(2)}) collective-permute-start(bf16[208,128]{1,0:T(8,128)(2,1)S(1)} %finish.6), channel_id=1, source_target_pairs={{0,4},{1,5},{2,6},{3,7},{4,0},{5,1},{6,2},{7,3},{8,12},{9,13},{10,... | collective-permute-start | bytes 159752 | tf_op jit(solution)/shard_map/ppermute | solution.py:63
  14.6 0.8 %finish.7.refs_3_ = bf16[208,128]{1,0:T(8,128)(2,1)S(1)} custom-call(f32[2,24,128]{2,1,0:T(8,128)S(1)} %get-tuple-element.17.frames_ref, bf16[768,128]{1,0:T(8,128)(2,1)S(1)} %get-tuple-element.23.queries_ref, f32[768,128]{1,0:T(8,128)S(1)} %get-tuple-element.24.sums_ref, f32[768,128]{1,0:T(8,128)S(1)} %get-tuple-element.25.stats_ref, ...), custom_call_target="tpu_custom_call" | custom-call | flops 113246208 | bytes 393216 | tf_op jit(solution)/shard_map/finish/pallas_call | solution.py:405
  15.4 3.1 %collective-permute-done.3.refs_1_ = bf16[208,128]{1,0:T(8,128)(2,1)S(1)} collective-permute-done((bf16[208,128]{1,0:T(8,128)(2,1)S(1)}, bf16[208,128]{1,0:T(8,128)(2,1)S(1)}, u32[]{:S(2)}, u32[]{:S(2)}) %collective-permute-start.3) | collective-permute-done | bytes 53280 | tf_op jit(solution)/shard_map/ppermute | solution.py:63
  18.5 0.5 collective-permute-done.4.refs_2_
  19.0 0.3 merge.2
  19.3 3.0 %collective-permute-start.6 = (bf16[208,128]{1,0:T(8,128)(2,1)S(1)}, bf16[208,128]{1,0:T(8,128)(2,1)S(1)}, u32[]{:S(2)}, u32[]{:S(2)}) collective-permute-start(bf16[208,128]{1,0:T(8,128)(2,1)S(1)} %merge.2), channel_id=1, source_target_pairs={{0,19},{1,18},{2,17},{3,16},{4,23},{5,22},{6,21},{7,20},{8,27},{9,... | collective-permute-start | bytes 159752 | tf_op jit(solution)/shard_map/ppermute | solution.py:78
  22.3 1.3 %collective-permute-start.5 = (bf16[208,128]{1,0:T(8,128)(2,1)S(1)}, bf16[208,128]{1,0:T(8,128)(2,1)S(1)}, u32[]{:S(2)}, u32[]{:S(2)}) collective-permute-start(bf16[208,128]{1,0:T(8,128)(2,1)S(1)} %merge.2), channel_id=1, source_target_pairs={{0,17},{1,16},{2,19},{3,18},{4,21},{5,20},{6,23},{7,22},{8,25},{9,... | collective-permute-start | bytes 159752 | tf_op jit(solution)/shard_map/ppermute | solution.py:78
  23.6 0.5 collective-permute-done.6.two_ref
  24.1 1.3 %collective-permute-done.5.one_ref = bf16[208,128]{1,0:T(8,128)(2,1)S(1)} collective-permute-done((bf16[208,128]{1,0:T(8,128)(2,1)S(1)}, bf16[208,128]{1,0:T(8,128)(2,1)S(1)}, u32[]{:S(2)}, u32[]{:S(2)}) %collective-permute-start.5) | collective-permute-done | bytes 53280 | tf_op jit(solution)/shard_map/ppermute | solution.py:78
  25.4 0.2 combine.2
  25.6 2.7 %collective-permute-start.7 = (bf16[24,1024]{1,0:T(8,128)(2,1)S(1)}, bf16[24,1024]{1,0:T(8,128)(2,1)S(1)}, u32[]{:S(2)}, u32[]{:S(2)}) collective-permute-start(bf16[24,1024]{1,0:T(8,128)(2,1)S(1)} %combine.2), channel_id=1, source_target_pairs={{0,13},{1,12},{2,15},{3,14},{4,9},{5,8},{6,11},{7,10},{8,5},{9,4},... | collective-permute-start | bytes 147464 | tf_op jit(solution)/shard_map/ppermute | solution.py:63
  28.4 1.9 %collective-permute-start.11 = (bf16[24,1024]{1,0:T(8,128)(2,1)S(1)}, bf16[24,1024]{1,0:T(8,128)(2,1)S(1)}, u32[]{:S(2)}, u32[]{:S(2)}) collective-permute-start(bf16[24,1024]{1,0:T(8,128)(2,1)S(1)} %combine.2), channel_id=1, source_target_pairs={{0,5},{1,4},{2,7},{3,6},{4,1},{5,0},{6,3},{7,2},{8,13},{9,12},{10,... | collective-permute-start | bytes 147464 | tf_op jit(solution)/shard_map/ppermute | solution.py:63
  30.3 0.7 %collective-permute-done.7.refs_4_ = bf16[24,1024]{1,0:T(8,128)(2,1)S(1)} collective-permute-done((bf16[24,1024]{1,0:T(8,128)(2,1)S(1)}, bf16[24,1024]{1,0:T(8,128)(2,1)S(1)}, u32[]{:S(2)}, u32[]{:S(2)}) %collective-permute-start.7) | collective-permute-done | bytes 49184 | tf_op jit(solution)/shard_map/ppermute | solution.py:63
  31.0 1.0 %partials.4 = bf16[208,128]{1,0:T(8,128)(2,1)S(1)} custom-call(f32[1,4096]{1,0:T(1,128)S(1)} %get-tuple-element.16.gain_ref, f32[2,24,128]{2,1,0:T(8,128)S(1)} %get-tuple-element.17.frames_ref, bf16[2,24,4096]{2,1,0:T(8,128)(2,1)S(1)} %get-tuple-element.18.batches_ref, bf16[784,512]{1,0:T(8,128)(2,1)S(1)} %get-tuple-element.19.keys_ref.refs_0_, ...), custom_call_target="tpu_custom_call" | custom-call | flops 226492416 | bytes 786432 | tf_op jit(solution)/shard_map/partials/pallas_call | solution.py:405
  32.0 3.1 %collective-permute-start.8 = (bf16[208,128]{1,0:T(8,128)(2,1)S(1)}, bf16[208,128]{1,0:T(8,128)(2,1)S(1)}, u32[]{:S(2)}, u32[]{:S(2)}) collective-permute-start(bf16[208,128]{1,0:T(8,128)(2,1)S(1)} %partials.4), channel_id=1, source_target_pairs={{0,13},{1,12},{2,15},{3,14},{4,9},{5,8},{6,11},{7,10},{8,5},{9,4},... | collective-permute-start | bytes 159752 | tf_op jit(solution)/shard_map/ppermute | solution.py:63
  35.1 1.0 %partials.5 = bf16[208,128]{1,0:T(8,128)(2,1)S(1)} custom-call(f32[1,4096]{1,0:T(1,128)S(1)} %get-tuple-element.16.gain_ref, f32[2,24,128]{2,1,0:T(8,128)S(1)} %get-tuple-element.17.frames_ref, bf16[2,24,4096]{2,1,0:T(8,128)(2,1)S(1)} %get-tuple-element.18.batches_ref, bf16[784,512]{1,0:T(8,128)(2,1)S(1)} %get-tuple-element.19.keys_ref.refs_0_, ...), custom_call_target="tpu_custom_call" | custom-call | flops 226492416 | bytes 786432 | tf_op jit(solution)/shard_map/partials/pallas_call | solution.py:405
  36.2 0.2 collective-permute-start.10
  36.4 1.0 %partials.6 = bf16[208,128]{1,0:T(8,128)(2,1)S(1)} custom-call(f32[1,4096]{1,0:T(1,128)S(1)} %get-tuple-element.16.gain_ref, f32[2,24,128]{2,1,0:T(8,128)S(1)} %get-tuple-element.17.frames_ref, bf16[2,24,4096]{2,1,0:T(8,128)(2,1)S(1)} %get-tuple-element.18.batches_ref, bf16[784,512]{1,0:T(8,128)(2,1)S(1)} %get-tuple-element.19.keys_ref.refs_0_, ...), custom_call_target="tpu_custom_call" | custom-call | flops 226492416 | bytes 786432 | tf_op jit(solution)/shard_map/partials/pallas_call | solution.py:405
  37.4 1.6 %collective-permute-start.12 = (bf16[208,128]{1,0:T(8,128)(2,1)S(1)}, bf16[208,128]{1,0:T(8,128)(2,1)S(1)}, u32[]{:S(2)}, u32[]{:S(2)}) collective-permute-start(bf16[208,128]{1,0:T(8,128)(2,1)S(1)} %partials.6), channel_id=1, source_target_pairs={{0,5},{1,4},{2,7},{3,6},{4,1},{5,0},{6,3},{7,2},{8,13},{9,12},{10,... | collective-permute-start | bytes 159752 | tf_op jit(solution)/shard_map/ppermute | solution.py:63
  39.0 1.0 %partials.7 = bf16[208,128]{1,0:T(8,128)(2,1)S(1)} custom-call(f32[1,4096]{1,0:T(1,128)S(1)} %get-tuple-element.16.gain_ref, f32[2,24,128]{2,1,0:T(8,128)S(1)} %get-tuple-element.17.frames_ref, bf16[2,24,4096]{2,1,0:T(8,128)(2,1)S(1)} %get-tuple-element.18.batches_ref, bf16[784,512]{1,0:T(8,128)(2,1)S(1)} %get-tuple-element.19.keys_ref.refs_0_, ...), custom_call_target="tpu_custom_call" | custom-call | flops 226492416 | bytes 786432 | tf_op jit(solution)/shard_map/partials/pallas_call | solution.py:405
  40.2 1.6 %collective-permute-done.10.refs_1_ = bf16[208,128]{1,0:T(8,128)(2,1)S(1)} collective-permute-done((bf16[208,128]{1,0:T(8,128)(2,1)S(1)}, bf16[208,128]{1,0:T(8,128)(2,1)S(1)}, u32[]{:S(2)}, u32[]{:S(2)}) %collective-permute-start.10) | collective-permute-done | bytes 53280 | tf_op jit(solution)/shard_map/ppermute | solution.py:63
  41.7 0.5 collective-permute-done.12.refs_2_
  42.2 0.3 merge.3
  42.5 0.2 collective-permute-start.16
  42.7 0.6 collective-permute-start.15
  43.2 3.3 %collective-permute-done.16.two_ref = bf16[208,128]{1,0:T(8,128)(2,1)S(1)} collective-permute-done((bf16[208,128]{1,0:T(8,128)(2,1)S(1)}, bf16[208,128]{1,0:T(8,128)(2,1)S(1)}, u32[]{:S(2)}, u32[]{:S(2)}) %collective-permute-start.16) | collective-permute-done | bytes 53280 | tf_op jit(solution)/shard_map/ppermute | solution.py:57
  46.5 0.2 combine.3.refs_0_
  46.8 1.7 %collective-permute-start.21 = (bf16[24,1024]{1,0:T(8,128)(2,1)S(1)}, bf16[24,1024]{1,0:T(8,128)(2,1)S(1)}, u32[]{:S(2)}, u32[]{:S(2)}) collective-permute-start(bf16[24,1024]{1,0:T(8,128)(2,1)S(1)} %combine.3.refs_0_), channel_id=1, source_target_pairs={{0,13},{1,12},{2,15},{3,14},{4,9},{5,8},{6,11},{7,10},{8,5},{9,4},... | collective-permute-start | bytes 147464 | tf_op jit(solution)/shard_map/ppermute | solution.py:63
  48.5 2.1 %collective-permute-start.17 = (bf16[24,1024]{1,0:T(8,128)(2,1)S(1)}, bf16[24,1024]{1,0:T(8,128)(2,1)S(1)}, u32[]{:S(2)}, u32[]{:S(2)}) collective-permute-start(bf16[24,1024]{1,0:T(8,128)(2,1)S(1)} %combine.3.refs_0_), channel_id=1, source_target_pairs={{0,5},{1,4},{2,7},{3,6},{4,1},{5,0},{6,3},{7,2},{8,13},{9,12},{10,... | collective-permute-start | bytes 147464 | tf_op jit(solution)/shard_map/ppermute | solution.py:63
  50.7 0.4 collective-permute-start.23
  51.1 1.3 %collective-permute-done.21.refs_7_ = bf16[24,1024]{1,0:T(8,128)(2,1)S(1)} collective-permute-done((bf16[24,1024]{1,0:T(8,128)(2,1)S(1)}, bf16[24,1024]{1,0:T(8,128)(2,1)S(1)}, u32[]{:S(2)}, u32[]{:S(2)}) %collective-permute-start.21) | collective-permute-done | bytes 49184 | tf_op jit(solution)/shard_map/ppermute | solution.py:63
  52.4 0.4 collective-permute-start.22
  52.9 1.9 %collective-permute-done.19.refs_6_ = bf16[24,1024]{1,0:T(8,128)(2,1)S(1)} collective-permute-done((bf16[24,1024]{1,0:T(8,128)(2,1)S(1)}, bf16[24,1024]{1,0:T(8,128)(2,1)S(1)}, u32[]{:S(2)}, u32[]{:S(2)}) %collective-permute-start.19) | collective-permute-done | bytes 49184 | tf_op jit(solution)/shard_map/ppermute | solution.py:63
  54.7 0.1 collective-permute-start.20
  54.9 0.4 collective-permute-start.18
  55.3 0.7 %collective-permute-done.20.refs_2_ = bf16[24,1024]{1,0:T(8,128)(2,1)S(1)} collective-permute-done((bf16[24,1024]{1,0:T(8,128)(2,1)S(1)}, bf16[24,1024]{1,0:T(8,128)(2,1)S(1)}, u32[]{:S(2)}, u32[]{:S(2)}) %collective-permute-start.20) | collective-permute-done | bytes 49184 | tf_op jit(solution)/shard_map/ppermute | solution.py:52
  56.0 0.2 collective-permute-done.18.refs_1_
  56.1 0.8 %assemble.1 = bf16[24,8192]{1,0:T(8,128)(2,1)} custom-call(bf16[24,1024]{1,0:T(8,128)(2,1)S(1)} %combine.3.refs_0_, bf16[24,1024]{1,0:T(8,128)(2,1)S(1)} %collective-permute-done.18.refs_1_, bf16[24,1024]{1,0:T(8,128)(2,1)S(1)} %collective-permute-done.20.refs_2_, bf16[24,1024]{1,0:T(8,128)(2,1)S(1)} %collective-permute-done.22.refs_3_, ...), custom_call_target="tpu_custom_call" | custom-call | tf_op jit(solution)/shard_map/assemble/pallas_call | solution.py:532
  (18 shorter events, 0.2 us)
Async XLA Ops:
  0.0 2.8 %copy-start = (bf16[1,768,1024]{2,1,0:T(8,128)(2,1)S(1)}, bf16[1,768,1024]{2,1,0:T(8,128)(2,1)}, u32[]{:S(2)}) copy-start(bf16[1,768,1024]{2,1,0:T(8,128)(2,1)} %param.14) | copy-start | bytes 4718596
  2.3 4.5 %collective-permute-start = (bf16[784,512]{1,0:T(8,128)(2,1)}, bf16[784,512]{1,0:T(8,128)(2,1)S(1)}, u32[]{:S(2)}, u32[]{:S(2)}) collective-permute-start(bf16[784,512]{1,0:T(8,128)(2,1)} %get-tuple-element.21), channel_id=1, source_target_pairs={{0,1},{1,0},{2,3},{3,2},{4,5},{5,4},{6,7},{7,6},{8,9},{9,8},{10,11... | collective-permute-start | bytes 2408456 | tf_op jit(solution)/shard_map/ppermute | solution.py:52
  4.3 2.6 %collective-permute-start.1 = (bf16[768,512]{1,0:T(8,128)(2,1)}, bf16[768,512]{1,0:T(8,128)(2,1)S(1)}, u32[]{:S(2)}, u32[]{:S(2)}) collective-permute-start(bf16[768,512]{1,0:T(8,128)(2,1)} %get-tuple-element.22), channel_id=1, source_target_pairs={{0,1},{1,0},{2,3},{3,2},{4,5},{5,4},{6,7},{7,6},{8,9},{9,8},{10,11... | collective-permute-start | bytes 2359304 | tf_op jit(solution)/shard_map/ppermute | solution.py:52
  7.6 7.8 %collective-permute-start.2 = (bf16[208,128]{1,0:T(8,128)(2,1)S(1)}, bf16[208,128]{1,0:T(8,128)(2,1)S(1)}, u32[]{:S(2)}, u32[]{:S(2)}) collective-permute-start(bf16[208,128]{1,0:T(8,128)(2,1)S(1)} %finish.4), channel_id=1, source_target_pairs={{0,12},{1,13},{2,14},{3,15},{4,8},{5,9},{6,10},{7,11},{8,4},{9,5},... | collective-permute-start | bytes 159752 | tf_op jit(solution)/shard_map/ppermute | solution.py:63
  13.1 5.3 %collective-permute-start.3 = (bf16[208,128]{1,0:T(8,128)(2,1)S(1)}, bf16[208,128]{1,0:T(8,128)(2,1)S(1)}, u32[]{:S(2)}, u32[]{:S(2)}) collective-permute-start(bf16[208,128]{1,0:T(8,128)(2,1)S(1)} %finish.5), channel_id=1, source_target_pairs={{0,8},{1,9},{2,10},{3,11},{4,12},{5,13},{6,14},{7,15},{8,0},{9,1},... | collective-permute-start | bytes 159752 | tf_op jit(solution)/shard_map/ppermute | solution.py:63
  14.0 5.0 %collective-permute-start.4 = (bf16[208,128]{1,0:T(8,128)(2,1)S(1)}, bf16[208,128]{1,0:T(8,128)(2,1)S(1)}, u32[]{:S(2)}, u32[]{:S(2)}) collective-permute-start(bf16[208,128]{1,0:T(8,128)(2,1)S(1)} %finish.6), channel_id=1, source_target_pairs={{0,4},{1,5},{2,6},{3,7},{4,0},{5,1},{6,2},{7,3},{8,12},{9,13},{10,... | collective-permute-start | bytes 159752 | tf_op jit(solution)/shard_map/ppermute | solution.py:63
  19.3 4.8 %collective-permute-start.6 = (bf16[208,128]{1,0:T(8,128)(2,1)S(1)}, bf16[208,128]{1,0:T(8,128)(2,1)S(1)}, u32[]{:S(2)}, u32[]{:S(2)}) collective-permute-start(bf16[208,128]{1,0:T(8,128)(2,1)S(1)} %merge.2), channel_id=1, source_target_pairs={{0,19},{1,18},{2,17},{3,16},{4,23},{5,22},{6,21},{7,20},{8,27},{9,... | collective-permute-start | bytes 159752 | tf_op jit(solution)/shard_map/ppermute | solution.py:78
  22.3 3.1 %collective-permute-start.5 = (bf16[208,128]{1,0:T(8,128)(2,1)S(1)}, bf16[208,128]{1,0:T(8,128)(2,1)S(1)}, u32[]{:S(2)}, u32[]{:S(2)}) collective-permute-start(bf16[208,128]{1,0:T(8,128)(2,1)S(1)} %merge.2), channel_id=1, source_target_pairs={{0,17},{1,16},{2,19},{3,18},{4,21},{5,20},{6,23},{7,22},{8,25},{9,... | collective-permute-start | bytes 159752 | tf_op jit(solution)/shard_map/ppermute | solution.py:78
  25.6 5.4 %collective-permute-start.7 = (bf16[24,1024]{1,0:T(8,128)(2,1)S(1)}, bf16[24,1024]{1,0:T(8,128)(2,1)S(1)}, u32[]{:S(2)}, u32[]{:S(2)}) collective-permute-start(bf16[24,1024]{1,0:T(8,128)(2,1)S(1)} %combine.2), channel_id=1, source_target_pairs={{0,13},{1,12},{2,15},{3,14},{4,9},{5,8},{6,11},{7,10},{8,5},{9,4},... | collective-permute-start | bytes 147464 | tf_op jit(solution)/shard_map/ppermute | solution.py:63
  28.4 6.8 %collective-permute-start.9 = (bf16[24,1024]{1,0:T(8,128)(2,1)S(1)}, bf16[24,1024]{1,0:T(8,128)(2,1)S(1)}, u32[]{:S(2)}, u32[]{:S(2)}) collective-permute-start(bf16[24,1024]{1,0:T(8,128)(2,1)S(1)} %combine.2), channel_id=1, source_target_pairs={{0,9},{1,8},{2,11},{3,10},{4,13},{5,12},{6,15},{7,14},{8,1},{9,0},... | collective-permute-start | bytes 147464 | tf_op jit(solution)/shard_map/ppermute | solution.py:63
  28.4 8.0 %collective-permute-start.11 = (bf16[24,1024]{1,0:T(8,128)(2,1)S(1)}, bf16[24,1024]{1,0:T(8,128)(2,1)S(1)}, u32[]{:S(2)}, u32[]{:S(2)}) collective-permute-start(bf16[24,1024]{1,0:T(8,128)(2,1)S(1)} %combine.2), channel_id=1, source_target_pairs={{0,5},{1,4},{2,7},{3,6},{4,1},{5,0},{6,3},{7,2},{8,13},{9,12},{10,... | collective-permute-start | bytes 147464 | tf_op jit(solution)/shard_map/ppermute | solution.py:63
  30.3 8.8 %collective-permute-start.13 = (bf16[24,1024]{1,0:T(8,128)(2,1)S(1)}, bf16[24,1024]{1,0:T(8,128)(2,1)S(1)}, u32[]{:S(2)}, u32[]{:S(2)}) collective-permute-start(bf16[24,1024]{1,0:T(8,128)(2,1)S(1)} %combine.2), channel_id=1, source_target_pairs={{0,1},{1,0},{2,3},{3,2},{4,5},{5,4},{6,7},{7,6},{8,9},{9,8},{10,11... | collective-permute-start | bytes 147464 | tf_op jit(solution)/shard_map/ppermute | solution.py:52
  32.0 8.1 %collective-permute-start.8 = (bf16[208,128]{1,0:T(8,128)(2,1)S(1)}, bf16[208,128]{1,0:T(8,128)(2,1)S(1)}, u32[]{:S(2)}, u32[]{:S(2)}) collective-permute-start(bf16[208,128]{1,0:T(8,128)(2,1)S(1)} %partials.4), channel_id=1, source_target_pairs={{0,13},{1,12},{2,15},{3,14},{4,9},{5,8},{6,11},{7,10},{8,5},{9,4},... | collective-permute-start | bytes 159752 | tf_op jit(solution)/shard_map/ppermute | solution.py:63
  36.2 5.6 %collective-permute-start.10 = (bf16[208,128]{1,0:T(8,128)(2,1)S(1)}, bf16[208,128]{1,0:T(8,128)(2,1)S(1)}, u32[]{:S(2)}, u32[]{:S(2)}) collective-permute-start(bf16[208,128]{1,0:T(8,128)(2,1)S(1)} %partials.5), channel_id=1, source_target_pairs={{0,9},{1,8},{2,11},{3,10},{4,13},{5,12},{6,15},{7,14},{8,1},{9,0},... | collective-permute-start | bytes 159752 | tf_op jit(solution)/shard_map/ppermute | solution.py:63
  37.4 4.8 %collective-permute-start.12 = (bf16[208,128]{1,0:T(8,128)(2,1)S(1)}, bf16[208,128]{1,0:T(8,128)(2,1)S(1)}, u32[]{:S(2)}, u32[]{:S(2)}) collective-permute-start(bf16[208,128]{1,0:T(8,128)(2,1)S(1)} %partials.6), channel_id=1, source_target_pairs={{0,5},{1,4},{2,7},{3,6},{4,1},{5,0},{6,3},{7,2},{8,13},{9,12},{10,... | collective-permute-start | bytes 159752 | tf_op jit(solution)/shard_map/ppermute | solution.py:63
  40.1 2.1 %collective-permute-start.14 = (bf16[208,128]{1,0:T(8,128)(2,1)S(1)}, bf16[208,128]{1,0:T(8,128)(2,1)S(1)}, u32[]{:S(2)}, u32[]{:S(2)}) collective-permute-start(bf16[208,128]{1,0:T(8,128)(2,1)S(1)} %partials.7), channel_id=1, source_target_pairs={{0,1},{1,0},{2,3},{3,2},{4,5},{5,4},{6,7},{7,6},{8,9},{9,8},{10,11... | collective-permute-start | bytes 159752 | tf_op jit(solution)/shard_map/ppermute | solution.py:52
  42.5 4.1 %collective-permute-start.16 = (bf16[208,128]{1,0:T(8,128)(2,1)S(1)}, bf16[208,128]{1,0:T(8,128)(2,1)S(1)}, u32[]{:S(2)}, u32[]{:S(2)}) collective-permute-start(bf16[208,128]{1,0:T(8,128)(2,1)S(1)} %merge.3), channel_id=1, source_target_pairs={{0,3},{1,2},{2,1},{3,0},{4,7},{5,6},{6,5},{7,4},{8,11},{9,10},{10,... | collective-permute-start | bytes 159752 | tf_op jit(solution)/shard_map/ppermute | solution.py:57
  42.7 3.9 %collective-permute-start.15 = (bf16[208,128]{1,0:T(8,128)(2,1)S(1)}, bf16[208,128]{1,0:T(8,128)(2,1)S(1)}, u32[]{:S(2)}, u32[]{:S(2)}) collective-permute-start(bf16[208,128]{1,0:T(8,128)(2,1)S(1)} %merge.3), channel_id=1, source_target_pairs={{0,1},{1,0},{2,3},{3,2},{4,5},{5,4},{6,7},{7,6},{8,9},{9,8},{10,11... | collective-permute-start | bytes 159752 | tf_op jit(solution)/shard_map/ppermute | solution.py:52
  46.8 5.7 %collective-permute-start.21 = (bf16[24,1024]{1,0:T(8,128)(2,1)S(1)}, bf16[24,1024]{1,0:T(8,128)(2,1)S(1)}, u32[]{:S(2)}, u32[]{:S(2)}) collective-permute-start(bf16[24,1024]{1,0:T(8,128)(2,1)S(1)} %combine.3.refs_0_), channel_id=1, source_target_pairs={{0,13},{1,12},{2,15},{3,14},{4,9},{5,8},{6,11},{7,10},{8,5},{9,4},... | collective-permute-start | bytes 147464 | tf_op jit(solution)/shard_map/ppermute | solution.py:63
  48.5 6.2 %collective-permute-start.19 = (bf16[24,1024]{1,0:T(8,128)(2,1)S(1)}, bf16[24,1024]{1,0:T(8,128)(2,1)S(1)}, u32[]{:S(2)}, u32[]{:S(2)}) collective-permute-start(bf16[24,1024]{1,0:T(8,128)(2,1)S(1)} %combine.3.refs_0_), channel_id=1, source_target_pairs={{0,9},{1,8},{2,11},{3,10},{4,13},{5,12},{6,15},{7,14},{8,1},{9,0},... | collective-permute-start | bytes 147464 | tf_op jit(solution)/shard_map/ppermute | solution.py:63
  48.5 6.3 %collective-permute-start.17 = (bf16[24,1024]{1,0:T(8,128)(2,1)S(1)}, bf16[24,1024]{1,0:T(8,128)(2,1)S(1)}, u32[]{:S(2)}, u32[]{:S(2)}) collective-permute-start(bf16[24,1024]{1,0:T(8,128)(2,1)S(1)} %combine.3.refs_0_), channel_id=1, source_target_pairs={{0,5},{1,4},{2,7},{3,6},{4,1},{5,0},{6,3},{7,2},{8,13},{9,12},{10,... | collective-permute-start | bytes 147464 | tf_op jit(solution)/shard_map/ppermute | solution.py:63
  50.7 4.6 %collective-permute-start.23 = (bf16[24,1024]{1,0:T(8,128)(2,1)S(1)}, bf16[24,1024]{1,0:T(8,128)(2,1)S(1)}, u32[]{:S(2)}, u32[]{:S(2)}) collective-permute-start(bf16[24,1024]{1,0:T(8,128)(2,1)S(1)} %combine.3.refs_0_), channel_id=1, source_target_pairs={{0,1},{1,0},{2,3},{3,2},{4,5},{5,4},{6,7},{7,6},{8,9},{9,8},{10,11... | collective-permute-start | bytes 147464 | tf_op jit(solution)/shard_map/ppermute | solution.py:52
  52.4 2.8 %collective-permute-start.22 = (bf16[24,1024]{1,0:T(8,128)(2,1)S(1)}, bf16[24,1024]{1,0:T(8,128)(2,1)S(1)}, u32[]{:S(2)}, u32[]{:S(2)}) collective-permute-start(bf16[24,1024]{1,0:T(8,128)(2,1)S(1)} %collective-permute-done.21.refs_7_), channel_id=1, source_target_pairs={{0,1},{1,0},{2,3},{3,2},{4,5},{5,4},{6,7},{7,6},{8,9},{9,8},{10,11... | collective-permute-start | bytes 147464 | tf_op jit(solution)/shard_map/ppermute | solution.py:52
  54.7 1.2 %collective-permute-start.20 = (bf16[24,1024]{1,0:T(8,128)(2,1)S(1)}, bf16[24,1024]{1,0:T(8,128)(2,1)S(1)}, u32[]{:S(2)}, u32[]{:S(2)}) collective-permute-start(bf16[24,1024]{1,0:T(8,128)(2,1)S(1)} %collective-permute-done.19.refs_6_), channel_id=1, source_target_pairs={{0,1},{1,0},{2,3},{3,2},{4,5},{5,4},{6,7},{7,6},{8,9},{9,8},{10,11... | collective-permute-start | bytes 147464 | tf_op jit(solution)/shard_map/ppermute | solution.py:52
  54.9 1.3 %collective-permute-start.18 = (bf16[24,1024]{1,0:T(8,128)(2,1)S(1)}, bf16[24,1024]{1,0:T(8,128)(2,1)S(1)}, u32[]{:S(2)}, u32[]{:S(2)}) collective-permute-start(bf16[24,1024]{1,0:T(8,128)(2,1)S(1)} %collective-permute-done.17.refs_5_), channel_id=1, source_target_pairs={{0,1},{1,0},{2,3},{3,2},{4,5},{5,4},{6,7},{7,6},{8,9},{9,8},{10,11... | collective-permute-start | bytes 147464 | tf_op jit(solution)/shard_map/ppermute | solution.py:52
where the time goes:
time: 57.1 us; the launch traced here: 56.9 us
  starting transfers between devices  26.1 us (46%)
  waiting for transfers between devices  16.7 us (29%)
  Pallas kernels  14 us (25%)
    ppermute x12, starting transfers between devices, from_outer(): lax.ppermute(block, 'ctx', [(i, i ^ INNER * PAIR * d ^ other_place) for i...  19 us
    ppermute x12, waiting for transfers between devices, from_outer(): lax.ppermute(block, 'ctx', [(i, i ^ INNER * PAIR * d ^ other_place) for i...  9.59 us
    pallas_call x8, Pallas kernels, chunk_call(): pl.pallas_call(functools.partial(kernel, d, kv_here), in_specs=[WHOLE] *...  7.18 us
    ppermute x2, starting transfers between devices, from_section_before(): return lax.ppermute(block, ('section', 'ctx'), route)  4.3 us
    ppermute x1, waiting for transfers between devices, from_inner(): return lax.ppermute(block, 'ctx', [(i, i ^ PAIR ^ 1) for i in range(size)])  3.32 us
    ppermute x9, starting transfers between devices, swapped(): lax.ppermute(block, 'ctx', [(i, i ^ 1) for i in range(lax.axis_size('ctx'...  2.63 us
    pallas_call x1, Pallas kernels, load_keys(): pl.pallas_call(load_keys_kernel, in_specs=[IN_HBM] * 2, out_specs=[WHOLE,...  2.27 us
    ppermute x9, waiting for transfers between devices, swapped(): lax.ppermute(block, 'ctx', [(i, i ^ 1) for i in range(lax.axis_size('ctx'...  2.01 us
  transfers between devices with their start and end apart: 24, of which 13 were waited for; matrix products, arithmetic and copies ran while one was open for 0% of the time, Pallas kernels for 16%

commit v1 on v0

--- a/solution.py
+++ b/solution.py
@@ -198,30 +198,24 @@
     return jnp.concatenate(values, axis=0), tops, totals
 
 
-def halve(staged_ref, copies, own_ref, given_ref, gift_ref, gift_sems, tail):
+def halve(staged_ref, copies, own_ref, given_ref, tail):
     length, width = staged_ref.shape
     half, step = width // PAIR, length // BLOCKS
     if tail is not None:
-        gift_ref[length:] = tail()
+        given_ref[length:] = tail()
         own_ref[length:] = tail()
     place = place_here()
-    gifts = []
     for b in range(BLOCKS):
         if copies:
             copies[b].wait()
         rows = pl.ds(b * step, step)
-        gift_ref[rows] = columns_of(1 - place, staged_ref.at[rows], half)[...]
+        given_ref[rows] = columns_of(1 - place, staged_ref.at[rows], half)[...]
         own_ref[rows] = columns_of(place, staged_ref.at[rows], half)[...]
-        if b == BLOCKS - 1:
-            rows = pl.ds(b * step, gift_ref.shape[0] - b * step)
-        gifts.append(pltpu.make_async_copy(gift_ref.at[rows], given_ref.at[rows], gift_sems.at[b]))
-        gifts[-1].start()
-    return gifts
 
 
 def load_keys_kernel(
     key_frames_in, keys_in, own_ref, given_ref,
-    key_frames_ref, staged_ref, gift_ref, sems, gift_sems, small_sem,
+    key_frames_ref, staged_ref, sems, small_sem,
 ):
     length, half = staged_ref.shape[0], own_ref.shape[1]
     small = pltpu.make_async_copy(key_frames_in, key_frames_ref, small_sem)
@@ -243,8 +237,7 @@
         copies.append(pltpu.make_async_copy(keys_in.at[rows], staged_ref.at[rows], sems.at[b]))
         copies[-1].start()
     small.wait()
-    for gift in halve(staged_ref, copies, own_ref, given_ref, gift_ref, gift_sems, tail):
-        gift.wait()
+    halve(staged_ref, copies, own_ref, given_ref, tail)
 
 
 def load_keys(key_frames, keys):
@@ -253,13 +246,11 @@
     return pl.pallas_call(
         load_keys_kernel,
         in_specs=[IN_HBM] * 2,
-        out_specs=[WHOLE, IN_HBM],
-        out_shape=[pltpu.VMEM(shape, keys.dtype), pltpu.HBM(shape, keys.dtype)],
+        out_specs=[WHOLE] * 2,
+        out_shape=[pltpu.VMEM(shape, keys.dtype)] * 2,
         scratch_shapes=[
             pltpu.VMEM(key_frames.shape, key_frames.dtype),
             pltpu.VMEM((length, width), keys.dtype),
-            pltpu.VMEM(shape, keys.dtype),
-            pltpu.SemaphoreType.DMA((BLOCKS,)),
             pltpu.SemaphoreType.DMA((BLOCKS,)),
             pltpu.SemaphoreType.DMA,
         ],
@@ -273,21 +264,23 @@
 
 def load_values_kernel(
     values_ref, act_frames_in, fresh_frames_in, batch_in, fresh_in, gain_in,
-    own_ref, given_ref, batches_ref, gain_ref, frames_ref,
-    act_frames_ref, fresh_frames_ref, gift_ref, gift_sems, small_sems,
+    own_ref, given_ref, batch_ref, gain_ref, fresh_ref, fresh_gain_ref, frames_ref,
+    act_frames_ref, fresh_frames_ref, small_sems,
 ):
-    place, half = place_here(), gain_ref.shape[1]
+    place, half, width = place_here(), gain_ref.shape[1], fresh_ref.shape[1]
+    share = (1 - place) * (half // width) + outer_here()
     small = [
         (act_frames_in, act_frames_ref),
         (fresh_frames_in, fresh_frames_ref),
-        (columns_of(place, batch_in, half), batches_ref.at[0]),
+        (columns_of(place, batch_in, half), batch_ref),
         (columns_of(place, gain_in, half), gain_ref),
-        (columns_of(place, fresh_in, half), batches_ref.at[1]),
+        (columns_of(share, fresh_in, width), fresh_ref),
+        (columns_of(share, gain_in, width), fresh_gain_ref),
     ]
     small = [pltpu.make_async_copy(a, b, small_sems.at[n]) for n, (a, b) in enumerate(small)]
     for copy in small:
         copy.start()
-    gifts = halve(values_ref, [], own_ref, given_ref, gift_ref, gift_sems, None)
+    halve(values_ref, [], own_ref, given_ref, None)
     for copy in small[:2]:
         copy.wait()
 
@@ -303,7 +296,7 @@
         column = jnp.sum(jnp.where(diagonal, row, 0.0), axis=1, keepdims=True)
         frames_ref[tick] = jnp.broadcast_to(column, (tokens, HD))
 
-    for copy in small[2:] + gifts:
+    for copy in small[2:]:
         copy.wait()
 
 
@@ -311,24 +304,25 @@
     length, width = values.shape
     tokens, model = batch.shape
     half = model // PAIR
+    share = half * INNER * PAIR // lax.axis_size("ctx")
     shape = (length, width // PAIR)
     return pl.pallas_call(
         load_values_kernel,
         in_specs=[WHOLE] + [IN_HBM] * 5,
-        out_specs=[WHOLE, IN_HBM] + [WHOLE] * 3,
+        out_specs=[WHOLE] * 7,
         out_shape=[
             pltpu.VMEM(shape, values.dtype),
-            pltpu.HBM(shape, values.dtype),
-            pltpu.VMEM((2, tokens, half), batch.dtype),
+            pltpu.VMEM(shape, values.dtype),
+            pltpu.VMEM((tokens, half), batch.dtype),
             pltpu.VMEM((1, half), gain.dtype),
+            pltpu.VMEM((tokens, share), fresh.dtype),
+            pltpu.VMEM((1, share), gain.dtype),
             pltpu.VMEM((2, tokens, HD), jnp.float32),
         ],
         scratch_shapes=[
             pltpu.VMEM(act_frames.shape, act_frames.dtype),
             pltpu.VMEM(fresh_frames.shape, fresh_frames.dtype),
-            pltpu.VMEM(shape, values.dtype),
-            pltpu.SemaphoreType.DMA((BLOCKS,)),
-            pltpu.SemaphoreType.DMA((5,)),
+            pltpu.SemaphoreType.DMA((6,)),
         ],
         cost_estimate=pl.CostEstimate(
             flops=0, bytes_accessed=2 * length * width, transcendentals=0
@@ -339,18 +333,18 @@
 
 
 def begin_kernel(
-    gain_ref, frames_ref, batches_ref, keys_ref, values_ref,
+    gain_ref, frames_ref, batch_ref, keys_ref, values_ref,
     queries_ref, sums_ref, stats_ref, share_ref,
 ):
     length = values_ref.shape[0]
     kv_here = values_ref.shape[1] // HD
     count, width = queries_ref.shape[0] // kv_here, gain_ref.shape[1] // kv_here
     bias = bias_of(keys_ref, frames_ref[0, :, :1])
-    share_ref[...] = columns_of(outer_here(), batches_ref.at[0], share_ref.shape[1])[...]
+    share_ref[...] = columns_of(outer_here(), batch_ref, share_ref.shape[1])[...]
     for g in range(kv_here):
         rows, columns = slice(g * count, (g + 1) * count), slice(g * width, (g + 1) * width)
         block = slice(g * HD, (g + 1) * HD)
-        queries = queries_of(batches_ref[0, :, columns], gain_ref[:, columns])
+        queries = queries_of(batch_ref[:, columns], gain_ref[:, columns])
         queries_ref[rows] = queries
         raw = scores(queries, keys_ref[:length, block], bias)
         top = top_of(raw)
@@ -360,9 +354,9 @@
         stats_ref[rows] = jnp.where(lane < HD // 2, top, both[:, HD:])
 
 
-def begin(gain, frames, batches, keys, values):
+def begin(gain, frames, batch, keys, values):
     length, width = values.shape
-    _, tokens, half = batches.shape
+    tokens, half = batch.shape
     queries = HEADS // PAIR * tokens
     return pl.pallas_call(
         begin_kernel,
@@ -372,7 +366,7 @@
             jax.ShapeDtypeStruct((queries, HD), jnp.bfloat16),
             jax.ShapeDtypeStruct((queries, HD), jnp.float32),
             jax.ShapeDtypeStruct((queries, HD), jnp.float32),
-            jax.ShapeDtypeStruct((tokens, half * HD // width), batches.dtype),
+            jax.ShapeDtypeStruct((tokens, half * HD // width), batch.dtype),
         ],
         cost_estimate=pl.CostEstimate(
             flops=2 * queries * length * 3 * HD,
@@ -381,7 +375,7 @@
         ),
         compiler_params=pltpu.CompilerParams(vmem_limit_bytes=16 * MIB),
         name="begin",
-    )(*in_vmem(gain, frames, batches, keys, values))
+    )(*in_vmem(gain, frames, batch, keys, values))
 
 
 def finish_kernel(
@@ -425,16 +419,13 @@
     return chunk_call(finish_kernel, "finish", d, kv_here, count, length, operands)
 
 
-def partials_kernel(d, kv_here, gain_ref, frames_ref, batches_ref, *refs):
-    kv_refs, (handed_ref, out_ref) = (refs[0:2], refs[2:4]), refs[4:]
-    length, width = kv_refs[0][1].shape[0], handed_ref.shape[1]
+def partials_kernel(d, kv_here, frames_ref, *refs):
+    kv_refs, (queries_ref, out_ref) = (refs[0:2], refs[2:4]), refs[4:]
+    length = kv_refs[0][1].shape[0]
     g = outer_here() ^ d
-    fresh = columns_of(g, batches_ref.at[1], width)[...].astype(jnp.float32)
-    x = jnp.where(in_first_section(), fresh, handed_ref[...].astype(jnp.float32))
-    queries = queries_of(x, columns_of(g, gain_ref, width)[...])
     raws = [
         scores(
-            queries,
+            queries_ref[...],
             columns_of(g, keys_ref.at[:length], HD)[...],
             bias_of(keys_ref, frames_ref[1, :, :1]),
         )
@@ -448,13 +439,11 @@
     write_sums(out_ref, both[:, :HD], top, both[:, HD:])
 
 
-def partials(d, gain, frames, batches, own, got, handed):
+def partials(d, frames, own, got, queries):
     length, width = own[1].shape
-    tokens = batches.shape[1]
-    count = handed.shape[1] // HD * tokens
-    operands = (gain, frames, batches, *own, *got, handed)
+    operands = (frames, *own, *got, queries)
     return chunk_call(
-        partials_kernel, "partials", d, width // HD, count, PAIR * length, operands
+        partials_kernel, "partials", d, width // HD, queries.shape[0], PAIR * length, operands
     )
 
 
@@ -480,41 +469,59 @@
     )(*in_vmem(*parts))
 
 
-def combined(one_ref, two_ref, x, out_ref):
+def attended(one_ref, two_ref):
     one, two = one_ref[...].astype(jnp.float32), two_ref[...].astype(jnp.float32)
     here = inner_here() == 0
     parts = [jnp.where(here, one, two), jnp.where(here, two, one)]
-    total, _, _ = joined([part.astype(jnp.bfloat16) for part in parts], True)
-    if x is not None:
-        total = head_rows(x) + total
-    tokens = out_ref.shape[0]
-    for h in range(total.shape[0] // tokens):
-        piece = total[h * tokens : (h + 1) * tokens]
-        out_ref[:, h * HD : (h + 1) * HD] = piece.astype(jnp.bfloat16)
-
-
-def combine_kernel(one_ref, two_ref, out_ref):
-    combined(one_ref, two_ref, None, out_ref)
-
-
-def combine_last_kernel(one_ref, two_ref, batches_ref, handed_ref, out_ref):
-    fresh = columns_of(outer_here(), batches_ref.at[1], out_ref.shape[1])[...]
-    x = jnp.where(
-        in_first_section(), fresh.astype(jnp.float32), handed_ref[...].astype(jnp.float32)
-    )
-    combined(one_ref, two_ref, x, out_ref)
-
-
-def combine(kernel, tokens, one, two, *rest):
-    width = (one.shape[0] - STAT_ROWS) // tokens * HD
-    return pl.pallas_call(
-        kernel,
-        in_specs=[WHOLE] * (2 + len(rest)),
-        out_specs=WHOLE,
-        out_shape=jax.ShapeDtypeStruct((tokens, width), jnp.bfloat16),
+    value, _, _ = joined([part.astype(jnp.bfloat16) for part in parts], True)
+    return value
+
+
+def columns_from(rows, tokens):
+    pieces = [rows[at : at + tokens] for at in range(0, rows.shape[0], tokens)]
+    return jnp.concatenate(pieces, axis=1)
+
+
+def combine_kernel(gain_ref, fresh_ref, one_ref, two_ref, share_ref, queries_ref):
+    tokens = fresh_ref.shape[0]
+    handed = columns_from(attended(one_ref, two_ref), tokens).astype(jnp.bfloat16)
+    fresh = fresh_ref[...].astype(jnp.float32)
+    share = jnp.where(in_first_section(), fresh, handed.astype(jnp.float32))
+    share = share.astype(jnp.bfloat16)
+    share_ref[...] = share
+    queries_ref[...] = queries_of(share, gain_ref[...])
+
+
+def combine(gain, fresh, one, two):
+    count = one.shape[0] - STAT_ROWS
+    return pl.pallas_call(
+        combine_kernel,
+        in_specs=[WHOLE] * 4,
+        out_specs=[WHOLE] * 2,
+        out_shape=[
+            jax.ShapeDtypeStruct(fresh.shape, fresh.dtype),
+            jax.ShapeDtypeStruct((count, HD), jnp.bfloat16),
+        ],
         compiler_params=pltpu.CompilerParams(vmem_limit_bytes=8 * MIB),
         name="combine",
-    )(*in_vmem(one, two, *rest))
+    )(*in_vmem(gain, fresh, one, two))
+
+
+def combine_last_kernel(share_ref, one_ref, two_ref, out_ref):
+    tokens = out_ref.shape[0]
+    total = head_rows(share_ref[...].astype(jnp.float32)) + attended(one_ref, two_ref)
+    out_ref[...] = columns_from(total, tokens).astype(jnp.bfloat16)
+
+
+def combine_last(share, one, two):
+    return pl.pallas_call(
+        combine_last_kernel,
+        in_specs=[WHOLE] * 3,
+        out_specs=WHOLE,
+        out_shape=jax.ShapeDtypeStruct(share.shape, share.dtype),
+        compiler_params=pltpu.CompilerParams(vmem_limit_bytes=8 * MIB),
+        name="combine_last",
+    )(*in_vmem(share, one, two))
 
 
 def assemble_kernel(*refs):
@@ -551,27 +558,24 @@
 ):
     own_keys, given_keys = load_keys(key_frames.reshape(-1, HD), cached_keys[0])
     got_keys = swapped(given_keys)
-    own_values, given_values, batches, gain, frames = load_values(
+    own_values, given_values, batch, gain, fresh, fresh_gain, frames = load_values(
         act_frames, fresh_frames[None], cached_values[0], activations[0], fresh_batch, norm_gain
     )
     got_values = swapped(given_values)
     own, got = (own_keys, own_values), (got_keys, got_values)
 
-    tokens = fresh_batch.shape[0]
     outers = lax.axis_size("ctx") // (INNER * PAIR)
-    *terms, share = begin(gain, frames, batches, *own)
+    *terms, share = begin(gain, frames, batch, *own)
     chunk, *others = [finish(d, frames, *terms, *got) for d in range(outers)]
     chunk = merge(merge_first_kernel, *from_outer(others, 0)[::-1], chunk, share)
     one, two = [from_section_before(chunk, step) for step in range(INNER)]
-    handed = combine(combine_kernel, tokens, one, two)
-    handed = [swapped(handed), *from_outer([handed] * len(others))]
-
-    chunk, *others = [
-        partials(d, gain, frames, batches, own, got, piece) for d, piece in enumerate(handed)
-    ]
+    share, queries = combine(fresh_gain, fresh, one, two)
+    queries = [swapped(queries), *from_outer([queries] * len(others))]
+
+    chunk, *others = [partials(d, frames, own, got, piece) for d, piece in enumerate(queries)]
     chunk = merge(merge_kernel, *from_outer(others)[::-1], swapped(chunk))
     one, two = swapped(chunk), from_inner(chunk)
-    share = combine(combine_last_kernel, tokens, one, two, batches, handed[0])
+    share = combine_last(swapped(share), one, two)
     theirs = [swapped(share), *from_outer([share] * len(others))]
     return assemble([share, *(swapped(piece) for piece in theirs[1:])], theirs)[None]
 

time: 57.1 us -> 55.6 us (0.974)
  Pallas kernels: 14 us -> 12.6 us
    ppermute x1, waiting for transfers between devices: 3.32 us -> 2 us  [from_inner(): return lax.ppermute(block, 'ctx', [(i, i ^ PAIR ^ 1) for i in range(size)])]
    ppermute x9 -> x10, waiting for transfers between devices: 2.01 us -> 2.79 us  [swapped(): lax.ppermute(block, 'ctx', [(i, i ^ 1) for i in range(lax.axis_size('ctx'...]
    pallas_call x3, Pallas kernels: 2.72 us -> 2.1 us  [the longest x1 1.55 us: load_keys(): pl.pallas_call(load_keys_kernel, in_specs=[IN_HBM] * 2, out_specs=[WHOLE]...]
    ppermute x9 -> x10, starting transfers between devices: 2.63 us -> 2.73 us  [swapped(): lax.ppermute(block, 'ctx', [(i, i ^ 1) for i in range(lax.axis_size('ctx'...]
  transfers between devices with their start and end apart: 24 -> 25, of which waited for: 13 -> 14; matrix products, arithmetic and copies ran while one was open for 0% -> 0% of each run, Pallas kernels for 16% -> 15%
where the time goes in v1:
time: 55.6 us; the launch traced here: 55.3 us
  starting transfers between devices  26.4 us (47%)
  waiting for transfers between devices  16.2 us (29%)
  Pallas kernels  12.6 us (23%)
    ppermute x12, starting transfers between devices, from_outer(): lax.ppermute(block, 'ctx', [(i, i ^ INNER * PAIR * d ^ other_place) for i...  19 us
    ppermute x12, waiting for transfers between devices, from_outer(): lax.ppermute(block, 'ctx', [(i, i ^ INNER * PAIR * d ^ other_place) for i...  9.67 us
    pallas_call x8, Pallas kernels, chunk_call(): pl.pallas_call(functools.partial(kernel, d, kv_here), in_specs=[WHOLE] *...  6.83 us
    ppermute x2, starting transfers between devices, from_section_before(): return lax.ppermute(block, ('section', 'ctx'), route)  4.36 us
    ppermute x10, waiting for transfers between devices, swapped(): lax.ppermute(block, 'ctx', [(i, i ^ 1) for i in range(lax.axis_size('ctx'...  2.79 us
    ppermute x10, starting transfers between devices, swapped(): lax.ppermute(block, 'ctx', [(i, i ^ 1) for i in range(lax.axis_size('ctx'...  2.73 us
    ppermute x1, waiting for transfers between devices, from_inner(): return lax.ppermute(block, 'ctx', [(i, i ^ PAIR ^ 1) for i in range(size)])  2 us
    ppermute x2, waiting for transfers between devices, from_section_before(): return lax.ppermute(block, ('section', 'ctx'), route)  1.77 us
  transfers between devices with their start and end apart: 25, of which 14 were waited for; matrix products, arithmetic and copies ran while one was open for 0% of the time, Pallas kernels for 15%

profile of v1, /device:TPU:0, one launch (start us, length us, event | category | flops | bytes accessed | tf_op | source)
XLA Modules:
  0.0 55.3 jit_solution(10056673547508264698)
XLA Ops:
  0.0 1.6 %load_keys.1 = (bf16[784,512]{1,0:T(8,128)(2,1)S(1)}, bf16[784,512]{1,0:T(8,128)(2,1)S(1)}) custom-call(s32[6,128]{1,0:T(8,128)} %bitcast.9, bf16[768,1024]{1,0:T(8,128)(2,1)} %bitcast.7), custom_call_target="tpu_custom_call" | custom-call | bytes 1572864 | tf_op jit(solution)/shard_map/load_keys/pallas_call | solution.py:246
  1.6 0.5 collective-permute-start
  2.1 1.0 %load_values.1 = (bf16[768,512]{1,0:T(8,128)(2,1)S(1)}, bf16[768,512]{1,0:T(8,128)(2,1)S(1)}, bf16[24,4096]{1,0:T(8,128)(2,1)S(1)}, f32[1,4096]{1,0:T(1,128)S(1)...) custom-call(bf16[768,1024]{1,0:T(8,128)(2,1)S(1)} %bitcast.6, ...), custom_call_target="tpu_custom_call" | custom-call | bytes 1572864 | tf_op jit(solution)/shard_map/load_values/pallas_call | solution.py:309
  3.1 0.3 collective-permute-start.1
  3.4 1.3 %begin.1 = (bf16[768,128]{1,0:T(8,128)(2,1)S(1)}, f32[768,128]{1,0:T(8,128)S(1)}, f32[768,128]{1,0:T(8,128)S(1)}, bf16[24,1024]{1,0:T(8,128)(2,1)S(1)}) custom-call(f32[1,4096]{1,0:T(1,128)S(1)} %get-tuple-element.23.gain_ref, f32[2,24,128]{2,1,0:T(8,128)S(1)} %get-tuple-element.22.frames_ref, bf16[24,4096]{1,0:T(8,128)(2,1)S(1)} %get-tuple-element.24.batch_ref, ...), custom_call_target="tpu_custom_call" | custom-call | flops 452984832 | bytes 1572864 | tf_op jit(solution)/shard_map/begin/pallas_call | solution.py:361
  4.8 0.7 %collective-permute-done.1.values_ref.refs_3_ = bf16[768,512]{1,0:T(8,128)(2,1)S(1)} collective-permute-done((bf16[768,512]{1,0:T(8,128)(2,1)S(1)}, bf16[768,512]{1,0:T(8,128)(2,1)S(1)}, u32[]{:S(2)}, u32[]{:S(2)}) %collective-permute-start.1) | collective-permute-done | bytes 786464 | tf_op jit(solution)/shard_map/ppermute | solution.py:52
  5.5 0.8 %finish.4 = bf16[208,128]{1,0:T(8,128)(2,1)S(1)} custom-call(f32[2,24,128]{2,1,0:T(8,128)S(1)} %get-tuple-element.22.frames_ref, bf16[768,128]{1,0:T(8,128)(2,1)S(1)} %get-tuple-element.27.queries_ref, f32[768,128]{1,0:T(8,128)S(1)} %get-tuple-element.28.sums_ref, f32[768,128]{1,0:T(8,128)S(1)} %get-tuple-element.29.stats_ref, ...), custom_call_target="tpu_custom_call" | custom-call | flops 113246208 | bytes 393216 | tf_op jit(solution)/shard_map/finish/pallas_call | solution.py:399
  6.2 4.9 %collective-permute-start.2 = (bf16[208,128]{1,0:T(8,128)(2,1)S(1)}, bf16[208,128]{1,0:T(8,128)(2,1)S(1)}, u32[]{:S(2)}, u32[]{:S(2)}) collective-permute-start(bf16[208,128]{1,0:T(8,128)(2,1)S(1)} %finish.4), channel_id=1, source_target_pairs={{0,12},{1,13},{2,14},{3,15},{4,8},{5,9},{6,10},{7,11},{8,4},{9,5},... | collective-permute-start | bytes 159752 | tf_op jit(solution)/shard_map/ppermute | solution.py:63
  11.1 0.7 %finish.5 = bf16[208,128]{1,0:T(8,128)(2,1)S(1)} custom-call(f32[2,24,128]{2,1,0:T(8,128)S(1)} %get-tuple-element.22.frames_ref, bf16[768,128]{1,0:T(8,128)(2,1)S(1)} %get-tuple-element.27.queries_ref, f32[768,128]{1,0:T(8,128)S(1)} %get-tuple-element.28.sums_ref, f32[768,128]{1,0:T(8,128)S(1)} %get-tuple-element.29.stats_ref, ...), custom_call_target="tpu_custom_call" | custom-call | flops 113246208 | bytes 393216 | tf_op jit(solution)/shard_map/finish/pallas_call | solution.py:399
  12.0 0.8 %finish.6 = bf16[208,128]{1,0:T(8,128)(2,1)S(1)} custom-call(f32[2,24,128]{2,1,0:T(8,128)S(1)} %get-tuple-element.22.frames_ref, bf16[768,128]{1,0:T(8,128)(2,1)S(1)} %get-tuple-element.27.queries_ref, f32[768,128]{1,0:T(8,128)S(1)} %get-tuple-element.28.sums_ref, f32[768,128]{1,0:T(8,128)S(1)} %get-tuple-element.29.stats_ref, ...), custom_call_target="tpu_custom_call" | custom-call | flops 113246208 | bytes 393216 | tf_op jit(solution)/shard_map/finish/pallas_call | solution.py:399
  12.7 0.6 %collective-permute-start.4 = (bf16[208,128]{1,0:T(8,128)(2,1)S(1)}, bf16[208,128]{1,0:T(8,128)(2,1)S(1)}, u32[]{:S(2)}, u32[]{:S(2)}) collective-permute-start(bf16[208,128]{1,0:T(8,128)(2,1)S(1)} %finish.6), channel_id=1, source_target_pairs={{0,4},{1,5},{2,6},{3,7},{4,0},{5,1},{6,2},{7,3},{8,12},{9,13},{10,... | collective-permute-start | bytes 159752 | tf_op jit(solution)/shard_map/ppermute | solution.py:63
  13.4 0.8 %finish.7.refs_3_ = bf16[208,128]{1,0:T(8,128)(2,1)S(1)} custom-call(f32[2,24,128]{2,1,0:T(8,128)S(1)} %get-tuple-element.22.frames_ref, bf16[768,128]{1,0:T(8,128)(2,1)S(1)} %get-tuple-element.27.queries_ref, f32[768,128]{1,0:T(8,128)S(1)} %get-tuple-element.28.sums_ref, f32[768,128]{1,0:T(8,128)S(1)} %get-tuple-element.29.stats_ref, ...), custom_call_target="tpu_custom_call" | custom-call | flops 113246208 | bytes 393216 | tf_op jit(solution)/shard_map/finish/pallas_call | solution.py:399
  14.1 3.1 %collective-permute-done.3.refs_1_ = bf16[208,128]{1,0:T(8,128)(2,1)S(1)} collective-permute-done((bf16[208,128]{1,0:T(8,128)(2,1)S(1)}, bf16[208,128]{1,0:T(8,128)(2,1)S(1)}, u32[]{:S(2)}, u32[]{:S(2)}) %collective-permute-start.3) | collective-permute-done | bytes 53280 | tf_op jit(solution)/shard_map/ppermute | solution.py:63
  17.2 0.5 collective-permute-done.4.refs_2_
  17.7 0.3 merge.2
  18.0 3.1 %collective-permute-start.6 = (bf16[208,128]{1,0:T(8,128)(2,1)S(1)}, bf16[208,128]{1,0:T(8,128)(2,1)S(1)}, u32[]{:S(2)}, u32[]{:S(2)}) collective-permute-start(bf16[208,128]{1,0:T(8,128)(2,1)S(1)} %merge.2), channel_id=1, source_target_pairs={{0,19},{1,18},{2,17},{3,16},{4,23},{5,22},{6,21},{7,20},{8,27},{9,... | collective-permute-start | bytes 159752 | tf_op jit(solution)/shard_map/ppermute | solution.py:78
  21.1 1.3 %collective-permute-start.5 = (bf16[208,128]{1,0:T(8,128)(2,1)S(1)}, bf16[208,128]{1,0:T(8,128)(2,1)S(1)}, u32[]{:S(2)}, u32[]{:S(2)}) collective-permute-start(bf16[208,128]{1,0:T(8,128)(2,1)S(1)} %merge.2), channel_id=1, source_target_pairs={{0,17},{1,16},{2,19},{3,18},{4,21},{5,20},{6,23},{7,22},{8,25},{9,... | collective-permute-start | bytes 159752 | tf_op jit(solution)/shard_map/ppermute | solution.py:78
  22.4 0.5 collective-permute-done.6.two_ref
  22.8 1.3 %collective-permute-done.5.one_ref = bf16[208,128]{1,0:T(8,128)(2,1)S(1)} collective-permute-done((bf16[208,128]{1,0:T(8,128)(2,1)S(1)}, bf16[208,128]{1,0:T(8,128)(2,1)S(1)}, u32[]{:S(2)}, u32[]{:S(2)}) %collective-permute-start.5) | collective-permute-done | bytes 53280 | tf_op jit(solution)/shard_map/ppermute | solution.py:78
  24.1 0.3 combine.1
  24.5 2.6 %collective-permute-start.8 = (bf16[192,128]{1,0:T(8,128)(2,1)S(1)}, bf16[192,128]{1,0:T(8,128)(2,1)S(1)}, u32[]{:S(2)}, u32[]{:S(2)}) collective-permute-start(bf16[192,128]{1,0:T(8,128)(2,1)S(1)} %get-tuple-element.34), channel_id=1, source_target_pairs={{0,13},{1,12},{2,15},{3,14},{4,9},{5,8},{6,11},{7,10},{8,5},{9,4},... | collective-permute-start | bytes 147464 | tf_op jit(solution)/shard_map/ppermute | solution.py:63
  27.2 1.9 %collective-permute-start.12 = (bf16[192,128]{1,0:T(8,128)(2,1)S(1)}, bf16[192,128]{1,0:T(8,128)(2,1)S(1)}, u32[]{:S(2)}, u32[]{:S(2)}) collective-permute-start(bf16[192,128]{1,0:T(8,128)(2,1)S(1)} %get-tuple-element.34), channel_id=1, source_target_pairs={{0,5},{1,4},{2,7},{3,6},{4,1},{5,0},{6,3},{7,2},{8,13},{9,12},{10,... | collective-permute-start | bytes 147464 | tf_op jit(solution)/shard_map/ppermute | solution.py:63
  29.1 0.8 %collective-permute-done.8.refs_4_ = bf16[192,128]{1,0:T(8,128)(2,1)S(1)} collective-permute-done((bf16[192,128]{1,0:T(8,128)(2,1)S(1)}, bf16[192,128]{1,0:T(8,128)(2,1)S(1)}, u32[]{:S(2)}, u32[]{:S(2)}) %collective-permute-start.8) | collective-permute-done | bytes 49184 | tf_op jit(solution)/shard_map/ppermute | solution.py:63
  29.8 0.9 %partials.4 = bf16[208,128]{1,0:T(8,128)(2,1)S(1)} custom-call(f32[2,24,128]{2,1,0:T(8,128)S(1)} %get-tuple-element.22.frames_ref, bf16[784,512]{1,0:T(8,128)(2,1)S(1)} %get-tuple-element.25.keys_ref.refs_0_, bf16[768,512]{1,0:T(8,128)(2,1)S(1)} %get-tuple-element.26.values_ref.refs_1_, bf16[784,512]{1,0:T(8,128)(2,1)S(1)} %collective-permute-done.keys_ref.refs_2_, ...), custom_call_target="tpu_custom_call" | custom-call | flops 226492416 | bytes 786432 | tf_op jit(solution)/shard_map/partials/pallas_call | solution.py:399
  30.8 3.0 %collective-permute-start.9 = (bf16[208,128]{1,0:T(8,128)(2,1)S(1)}, bf16[208,128]{1,0:T(8,128)(2,1)S(1)}, u32[]{:S(2)}, u32[]{:S(2)}) collective-permute-start(bf16[208,128]{1,0:T(8,128)(2,1)S(1)} %partials.4), channel_id=1, source_target_pairs={{0,13},{1,12},{2,15},{3,14},{4,9},{5,8},{6,11},{7,10},{8,5},{9,4},... | collective-permute-start | bytes 159752 | tf_op jit(solution)/shard_map/ppermute | solution.py:63
  33.8 0.9 %partials.5 = bf16[208,128]{1,0:T(8,128)(2,1)S(1)} custom-call(f32[2,24,128]{2,1,0:T(8,128)S(1)} %get-tuple-element.22.frames_ref, bf16[784,512]{1,0:T(8,128)(2,1)S(1)} %get-tuple-element.25.keys_ref.refs_0_, bf16[768,512]{1,0:T(8,128)(2,1)S(1)} %get-tuple-element.26.values_ref.refs_1_, bf16[784,512]{1,0:T(8,128)(2,1)S(1)} %collective-permute-done.keys_ref.refs_2_, ...), custom_call_target="tpu_custom_call" | custom-call | flops 226492416 | bytes 786432 | tf_op jit(solution)/shard_map/partials/pallas_call | solution.py:399
  34.7 0.5 collective-permute-start.11
  35.2 1.0 %partials.6 = bf16[208,128]{1,0:T(8,128)(2,1)S(1)} custom-call(f32[2,24,128]{2,1,0:T(8,128)S(1)} %get-tuple-element.22.frames_ref, bf16[784,512]{1,0:T(8,128)(2,1)S(1)} %get-tuple-element.25.keys_ref.refs_0_, bf16[768,512]{1,0:T(8,128)(2,1)S(1)} %get-tuple-element.26.values_ref.refs_1_, bf16[784,512]{1,0:T(8,128)(2,1)S(1)} %collective-permute-done.keys_ref.refs_2_, ...), custom_call_target="tpu_custom_call" | custom-call | flops 226492416 | bytes 786432 | tf_op jit(solution)/shard_map/partials/pallas_call | solution.py:399
  36.2 1.4 %collective-permute-start.13 = (bf16[208,128]{1,0:T(8,128)(2,1)S(1)}, bf16[208,128]{1,0:T(8,128)(2,1)S(1)}, u32[]{:S(2)}, u32[]{:S(2)}) collective-permute-start(bf16[208,128]{1,0:T(8,128)(2,1)S(1)} %partials.6), channel_id=1, source_target_pairs={{0,5},{1,4},{2,7},{3,6},{4,1},{5,0},{6,3},{7,2},{8,13},{9,12},{10,... | collective-permute-start | bytes 159752 | tf_op jit(solution)/shard_map/ppermute | solution.py:63
  37.6 1.0 %partials.7 = bf16[208,128]{1,0:T(8,128)(2,1)S(1)} custom-call(f32[2,24,128]{2,1,0:T(8,128)S(1)} %get-tuple-element.22.frames_ref, bf16[784,512]{1,0:T(8,128)(2,1)S(1)} %get-tuple-element.25.keys_ref.refs_0_, bf16[768,512]{1,0:T(8,128)(2,1)S(1)} %get-tuple-element.26.values_ref.refs_1_, bf16[784,512]{1,0:T(8,128)(2,1)S(1)} %collective-permute-done.keys_ref.refs_2_, ...), custom_call_target="tpu_custom_call" | custom-call | flops 226492416 | bytes 786432 | tf_op jit(solution)/shard_map/partials/pallas_call | solution.py:399
  38.6 1.6 %collective-permute-done.11.refs_1_ = bf16[208,128]{1,0:T(8,128)(2,1)S(1)} collective-permute-done((bf16[208,128]{1,0:T(8,128)(2,1)S(1)}, bf16[208,128]{1,0:T(8,128)(2,1)S(1)}, u32[]{:S(2)}, u32[]{:S(2)}) %collective-permute-start.11) | collective-permute-done | bytes 53280 | tf_op jit(solution)/shard_map/ppermute | solution.py:63
  40.3 0.5 collective-permute-done.13.refs_2_
  40.7 0.3 merge.3
  41.0 0.3 collective-permute-start.17
  41.3 0.5 collective-permute-start.16
  41.8 1.2 %collective-permute-done.7.share_ref = bf16[24,1024]{1,0:T(8,128)(2,1)S(1)} collective-permute-done((bf16[24,1024]{1,0:T(8,128)(2,1)S(1)}, bf16[24,1024]{1,0:T(8,128)(2,1)S(1)}, u32[]{:S(2)}, u32[]{:S(2)}) %collective-permute-start.7) | collective-permute-done | bytes 49184 | tf_op jit(solution)/shard_map/ppermute | solution.py:52
  43.0 2.0 %collective-permute-done.17.two_ref = bf16[208,128]{1,0:T(8,128)(2,1)S(1)} collective-permute-done((bf16[208,128]{1,0:T(8,128)(2,1)S(1)}, bf16[208,128]{1,0:T(8,128)(2,1)S(1)}, u32[]{:S(2)}, u32[]{:S(2)}) %collective-permute-start.17) | collective-permute-done | bytes 53280 | tf_op jit(solution)/shard_map/ppermute | solution.py:57
  45.0 0.2 combine_last.1.refs_0_
  45.2 1.7 %collective-permute-start.22 = (bf16[24,1024]{1,0:T(8,128)(2,1)S(1)}, bf16[24,1024]{1,0:T(8,128)(2,1)S(1)}, u32[]{:S(2)}, u32[]{:S(2)}) collective-permute-start(bf16[24,1024]{1,0:T(8,128)(2,1)S(1)} %combine_last.1.refs_0_), channel_id=1, source_target_pairs={{0,13},{1,12},{2,15},{3,14},{4,9},{5,8},{6,11},{7,10},{8,5},{9,4},... | collective-permute-start | bytes 147464 | tf_op jit(solution)/shard_map/ppermute | solution.py:63
  47.0 2.2 %collective-permute-start.18 = (bf16[24,1024]{1,0:T(8,128)(2,1)S(1)}, bf16[24,1024]{1,0:T(8,128)(2,1)S(1)}, u32[]{:S(2)}, u32[]{:S(2)}) collective-permute-start(bf16[24,1024]{1,0:T(8,128)(2,1)S(1)} %combine_last.1.refs_0_), channel_id=1, source_target_pairs={{0,5},{1,4},{2,7},{3,6},{4,1},{5,0},{6,3},{7,2},{8,13},{9,12},{10,... | collective-permute-start | bytes 147464 | tf_op jit(solution)/shard_map/ppermute | solution.py:63
  49.1 0.4 collective-permute-start.24
  49.5 1.4 %collective-permute-done.22.refs_7_ = bf16[24,1024]{1,0:T(8,128)(2,1)S(1)} collective-permute-done((bf16[24,1024]{1,0:T(8,128)(2,1)S(1)}, bf16[24,1024]{1,0:T(8,128)(2,1)S(1)}, u32[]{:S(2)}, u32[]{:S(2)}) %collective-permute-start.22) | collective-permute-done | bytes 49184 | tf_op jit(solution)/shard_map/ppermute | solution.py:63
  50.9 0.4 collective-permute-start.23
  51.3 1.9 %collective-permute-done.20.refs_6_ = bf16[24,1024]{1,0:T(8,128)(2,1)S(1)} collective-permute-done((bf16[24,1024]{1,0:T(8,128)(2,1)S(1)}, bf16[24,1024]{1,0:T(8,128)(2,1)S(1)}, u32[]{:S(2)}, u32[]{:S(2)}) %collective-permute-start.20) | collective-permute-done | bytes 49184 | tf_op jit(solution)/shard_map/ppermute | solution.py:63
  53.3 0.4 collective-permute-start.19
  53.7 0.7 %collective-permute-done.21.refs_2_ = bf16[24,1024]{1,0:T(8,128)(2,1)S(1)} collective-permute-done((bf16[24,1024]{1,0:T(8,128)(2,1)S(1)}, bf16[24,1024]{1,0:T(8,128)(2,1)S(1)}, u32[]{:S(2)}, u32[]{:S(2)}) %collective-permute-start.21) | collective-permute-done | bytes 49184 | tf_op jit(solution)/shard_map/ppermute | solution.py:52
  54.4 0.2 collective-permute-done.19.refs_1_
  54.6 0.8 %assemble.1 = bf16[24,8192]{1,0:T(8,128)(2,1)} custom-call(bf16[24,1024]{1,0:T(8,128)(2,1)S(1)} %combine_last.1.refs_0_, bf16[24,1024]{1,0:T(8,128)(2,1)S(1)} %collective-permute-done.19.refs_1_, bf16[24,1024]{1,0:T(8,128)(2,1)S(1)} %collective-permute-done.21.refs_2_, bf16[24,1024]{1,0:T(8,128)(2,1)S(1)} %collective-permute-done.23.refs_3_, ...), custom_call_target="tpu_custom_call" | custom-call | tf_op jit(solution)/shard_map/assemble/pallas_call | solution.py:539
  (20 shorter events, 0.5 us)
Async XLA Ops:
  0.0 2.1 %copy-start = (bf16[1,768,1024]{2,1,0:T(8,128)(2,1)S(1)}, bf16[1,768,1024]{2,1,0:T(8,128)(2,1)}, u32[]{:S(2)}) copy-start(bf16[1,768,1024]{2,1,0:T(8,128)(2,1)} %param.14) | copy-start | bytes 4718596
  1.6 3.9 %collective-permute-start = (bf16[784,512]{1,0:T(8,128)(2,1)S(1)}, bf16[784,512]{1,0:T(8,128)(2,1)S(1)}, u32[]{:S(2)}, u32[]{:S(2)}) collective-permute-start(bf16[784,512]{1,0:T(8,128)(2,1)S(1)} %get-tuple-element.30), channel_id=1, source_target_pairs={{0,1},{1,0},{2,3},{3,2},{4,5},{5,4},{6,7},{7,6},{8,9},{9,8},{10,11... | collective-permute-start | bytes 2408456 | tf_op jit(solution)/shard_map/ppermute | solution.py:52
  3.1 2.4 %collective-permute-start.1 = (bf16[768,512]{1,0:T(8,128)(2,1)S(1)}, bf16[768,512]{1,0:T(8,128)(2,1)S(1)}, u32[]{:S(2)}, u32[]{:S(2)}) collective-permute-start(bf16[768,512]{1,0:T(8,128)(2,1)S(1)} %get-tuple-element.31), channel_id=1, source_target_pairs={{0,1},{1,0},{2,3},{3,2},{4,5},{5,4},{6,7},{7,6},{8,9},{9,8},{10,11... | collective-permute-start | bytes 2359304 | tf_op jit(solution)/shard_map/ppermute | solution.py:52
  6.2 7.9 %collective-permute-start.2 = (bf16[208,128]{1,0:T(8,128)(2,1)S(1)}, bf16[208,128]{1,0:T(8,128)(2,1)S(1)}, u32[]{:S(2)}, u32[]{:S(2)}) collective-permute-start(bf16[208,128]{1,0:T(8,128)(2,1)S(1)} %finish.4), channel_id=1, source_target_pairs={{0,12},{1,13},{2,14},{3,15},{4,8},{5,9},{6,10},{7,11},{8,4},{9,5},... | collective-permute-start | bytes 159752 | tf_op jit(solution)/shard_map/ppermute | solution.py:63
  11.9 5.3 %collective-permute-start.3 = (bf16[208,128]{1,0:T(8,128)(2,1)S(1)}, bf16[208,128]{1,0:T(8,128)(2,1)S(1)}, u32[]{:S(2)}, u32[]{:S(2)}) collective-permute-start(bf16[208,128]{1,0:T(8,128)(2,1)S(1)} %finish.5), channel_id=1, source_target_pairs={{0,8},{1,9},{2,10},{3,11},{4,12},{5,13},{6,14},{7,15},{8,0},{9,1},... | collective-permute-start | bytes 159752 | tf_op jit(solution)/shard_map/ppermute | solution.py:63
  12.7 4.9 %collective-permute-start.4 = (bf16[208,128]{1,0:T(8,128)(2,1)S(1)}, bf16[208,128]{1,0:T(8,128)(2,1)S(1)}, u32[]{:S(2)}, u32[]{:S(2)}) collective-permute-start(bf16[208,128]{1,0:T(8,128)(2,1)S(1)} %finish.6), channel_id=1, source_target_pairs={{0,4},{1,5},{2,6},{3,7},{4,0},{5,1},{6,2},{7,3},{8,12},{9,13},{10,... | collective-permute-start | bytes 159752 | tf_op jit(solution)/shard_map/ppermute | solution.py:63
  18.0 4.8 %collective-permute-start.6 = (bf16[208,128]{1,0:T(8,128)(2,1)S(1)}, bf16[208,128]{1,0:T(8,128)(2,1)S(1)}, u32[]{:S(2)}, u32[]{:S(2)}) collective-permute-start(bf16[208,128]{1,0:T(8,128)(2,1)S(1)} %merge.2), channel_id=1, source_target_pairs={{0,19},{1,18},{2,17},{3,16},{4,23},{5,22},{6,21},{7,20},{8,27},{9,... | collective-permute-start | bytes 159752 | tf_op jit(solution)/shard_map/ppermute | solution.py:78
  21.1 3.1 %collective-permute-start.5 = (bf16[208,128]{1,0:T(8,128)(2,1)S(1)}, bf16[208,128]{1,0:T(8,128)(2,1)S(1)}, u32[]{:S(2)}, u32[]{:S(2)}) collective-permute-start(bf16[208,128]{1,0:T(8,128)(2,1)S(1)} %merge.2), channel_id=1, source_target_pairs={{0,17},{1,16},{2,19},{3,18},{4,21},{5,20},{6,23},{7,22},{8,25},{9,... | collective-permute-start | bytes 159752 | tf_op jit(solution)/shard_map/ppermute | solution.py:78
  24.5 5.4 %collective-permute-start.8 = (bf16[192,128]{1,0:T(8,128)(2,1)S(1)}, bf16[192,128]{1,0:T(8,128)(2,1)S(1)}, u32[]{:S(2)}, u32[]{:S(2)}) collective-permute-start(bf16[192,128]{1,0:T(8,128)(2,1)S(1)} %get-tuple-element.34), channel_id=1, source_target_pairs={{0,13},{1,12},{2,15},{3,14},{4,9},{5,8},{6,11},{7,10},{8,5},{9,4},... | collective-permute-start | bytes 147464 | tf_op jit(solution)/shard_map/ppermute | solution.py:63
  27.0 6.7 %collective-permute-start.10 = (bf16[192,128]{1,0:T(8,128)(2,1)S(1)}, bf16[192,128]{1,0:T(8,128)(2,1)S(1)}, u32[]{:S(2)}, u32[]{:S(2)}) collective-permute-start(bf16[192,128]{1,0:T(8,128)(2,1)S(1)} %get-tuple-element.34), channel_id=1, source_target_pairs={{0,9},{1,8},{2,11},{3,10},{4,13},{5,12},{6,15},{7,14},{8,1},{9,0},... | collective-permute-start | bytes 147464 | tf_op jit(solution)/shard_map/ppermute | solution.py:63
  27.2 8.0 %collective-permute-start.12 = (bf16[192,128]{1,0:T(8,128)(2,1)S(1)}, bf16[192,128]{1,0:T(8,128)(2,1)S(1)}, u32[]{:S(2)}, u32[]{:S(2)}) collective-permute-start(bf16[192,128]{1,0:T(8,128)(2,1)S(1)} %get-tuple-element.34), channel_id=1, source_target_pairs={{0,5},{1,4},{2,7},{3,6},{4,1},{5,0},{6,3},{7,2},{8,13},{9,12},{10,... | collective-permute-start | bytes 147464 | tf_op jit(solution)/shard_map/ppermute | solution.py:63
  29.1 8.5 %collective-permute-start.14 = (bf16[192,128]{1,0:T(8,128)(2,1)S(1)}, bf16[192,128]{1,0:T(8,128)(2,1)S(1)}, u32[]{:S(2)}, u32[]{:S(2)}) collective-permute-start(bf16[192,128]{1,0:T(8,128)(2,1)S(1)} %get-tuple-element.34), channel_id=1, source_target_pairs={{0,1},{1,0},{2,3},{3,2},{4,5},{5,4},{6,7},{7,6},{8,9},{9,8},{10,11... | collective-permute-start | bytes 147464 | tf_op jit(solution)/shard_map/ppermute | solution.py:52
  30.8 7.8 %collective-permute-start.9 = (bf16[208,128]{1,0:T(8,128)(2,1)S(1)}, bf16[208,128]{1,0:T(8,128)(2,1)S(1)}, u32[]{:S(2)}, u32[]{:S(2)}) collective-permute-start(bf16[208,128]{1,0:T(8,128)(2,1)S(1)} %partials.4), channel_id=1, source_target_pairs={{0,13},{1,12},{2,15},{3,14},{4,9},{5,8},{6,11},{7,10},{8,5},{9,4},... | collective-permute-start | bytes 159752 | tf_op jit(solution)/shard_map/ppermute | solution.py:63
  34.7 5.6 %collective-permute-start.11 = (bf16[208,128]{1,0:T(8,128)(2,1)S(1)}, bf16[208,128]{1,0:T(8,128)(2,1)S(1)}, u32[]{:S(2)}, u32[]{:S(2)}) collective-permute-start(bf16[208,128]{1,0:T(8,128)(2,1)S(1)} %partials.5), channel_id=1, source_target_pairs={{0,9},{1,8},{2,11},{3,10},{4,13},{5,12},{6,15},{7,14},{8,1},{9,0},... | collective-permute-start | bytes 159752 | tf_op jit(solution)/shard_map/ppermute | solution.py:63
  36.2 4.5 %collective-permute-start.13 = (bf16[208,128]{1,0:T(8,128)(2,1)S(1)}, bf16[208,128]{1,0:T(8,128)(2,1)S(1)}, u32[]{:S(2)}, u32[]{:S(2)}) collective-permute-start(bf16[208,128]{1,0:T(8,128)(2,1)S(1)} %partials.6), channel_id=1, source_target_pairs={{0,5},{1,4},{2,7},{3,6},{4,1},{5,0},{6,3},{7,2},{8,13},{9,12},{10,... | collective-permute-start | bytes 159752 | tf_op jit(solution)/shard_map/ppermute | solution.py:63
  38.5 2.2 %collective-permute-start.15 = (bf16[208,128]{1,0:T(8,128)(2,1)S(1)}, bf16[208,128]{1,0:T(8,128)(2,1)S(1)}, u32[]{:S(2)}, u32[]{:S(2)}) collective-permute-start(bf16[208,128]{1,0:T(8,128)(2,1)S(1)} %partials.7), channel_id=1, source_target_pairs={{0,1},{1,0},{2,3},{3,2},{4,5},{5,4},{6,7},{7,6},{8,9},{9,8},{10,11... | collective-permute-start | bytes 159752 | tf_op jit(solution)/shard_map/ppermute | solution.py:52
  41.0 4.0 %collective-permute-start.17 = (bf16[208,128]{1,0:T(8,128)(2,1)S(1)}, bf16[208,128]{1,0:T(8,128)(2,1)S(1)}, u32[]{:S(2)}, u32[]{:S(2)}) collective-permute-start(bf16[208,128]{1,0:T(8,128)(2,1)S(1)} %merge.3), channel_id=1, source_target_pairs={{0,3},{1,2},{2,1},{3,0},{4,7},{5,6},{6,5},{7,4},{8,11},{9,10},{10,... | collective-permute-start | bytes 159752 | tf_op jit(solution)/shard_map/ppermute | solution.py:57
  41.3 3.7 %collective-permute-start.16 = (bf16[208,128]{1,0:T(8,128)(2,1)S(1)}, bf16[208,128]{1,0:T(8,128)(2,1)S(1)}, u32[]{:S(2)}, u32[]{:S(2)}) collective-permute-start(bf16[208,128]{1,0:T(8,128)(2,1)S(1)} %merge.3), channel_id=1, source_target_pairs={{0,1},{1,0},{2,3},{3,2},{4,5},{5,4},{6,7},{7,6},{8,9},{9,8},{10,11... | collective-permute-start | bytes 159752 | tf_op jit(solution)/shard_map/ppermute | solution.py:52
  41.7 1.2 %collective-permute-start.7 = (bf16[24,1024]{1,0:T(8,128)(2,1)S(1)}, bf16[24,1024]{1,0:T(8,128)(2,1)S(1)}, u32[]{:S(2)}, u32[]{:S(2)}) collective-permute-start(bf16[24,1024]{1,0:T(8,128)(2,1)S(1)} %get-tuple-element.33), channel_id=1, source_target_pairs={{0,1},{1,0},{2,3},{3,2},{4,5},{5,4},{6,7},{7,6},{8,9},{9,8},{10,11... | collective-permute-start | bytes 147464 | tf_op jit(solution)/shard_map/ppermute | solution.py:52
  45.2 5.7 %collective-permute-start.22 = (bf16[24,1024]{1,0:T(8,128)(2,1)S(1)}, bf16[24,1024]{1,0:T(8,128)(2,1)S(1)}, u32[]{:S(2)}, u32[]{:S(2)}) collective-permute-start(bf16[24,1024]{1,0:T(8,128)(2,1)S(1)} %combine_last.1.refs_0_), channel_id=1, source_target_pairs={{0,13},{1,12},{2,15},{3,14},{4,9},{5,8},{6,11},{7,10},{8,5},{9,4},... | collective-permute-start | bytes 147464 | tf_op jit(solution)/shard_map/ppermute | solution.py:63
  46.9 6.2 %collective-permute-start.20 = (bf16[24,1024]{1,0:T(8,128)(2,1)S(1)}, bf16[24,1024]{1,0:T(8,128)(2,1)S(1)}, u32[]{:S(2)}, u32[]{:S(2)}) collective-permute-start(bf16[24,1024]{1,0:T(8,128)(2,1)S(1)} %combine_last.1.refs_0_), channel_id=1, source_target_pairs={{0,9},{1,8},{2,11},{3,10},{4,13},{5,12},{6,15},{7,14},{8,1},{9,0},... | collective-permute-start | bytes 147464 | tf_op jit(solution)/shard_map/ppermute | solution.py:63
  47.0 6.3 %collective-permute-start.18 = (bf16[24,1024]{1,0:T(8,128)(2,1)S(1)}, bf16[24,1024]{1,0:T(8,128)(2,1)S(1)}, u32[]{:S(2)}, u32[]{:S(2)}) collective-permute-start(bf16[24,1024]{1,0:T(8,128)(2,1)S(1)} %combine_last.1.refs_0_), channel_id=1, source_target_pairs={{0,5},{1,4},{2,7},{3,6},{4,1},{5,0},{6,3},{7,2},{8,13},{9,12},{10,... | collective-permute-start | bytes 147464 | tf_op jit(solution)/shard_map/ppermute | solution.py:63
  49.1 4.6 %collective-permute-start.24 = (bf16[24,1024]{1,0:T(8,128)(2,1)S(1)}, bf16[24,1024]{1,0:T(8,128)(2,1)S(1)}, u32[]{:S(2)}, u32[]{:S(2)}) collective-permute-start(bf16[24,1024]{1,0:T(8,128)(2,1)S(1)} %combine_last.1.refs_0_), channel_id=1, source_target_pairs={{0,1},{1,0},{2,3},{3,2},{4,5},{5,4},{6,7},{7,6},{8,9},{9,8},{10,11... | collective-permute-start | bytes 147464 | tf_op jit(solution)/shard_map/ppermute | solution.py:52
  50.9 2.8 %collective-permute-start.23 = (bf16[24,1024]{1,0:T(8,128)(2,1)S(1)}, bf16[24,1024]{1,0:T(8,128)(2,1)S(1)}, u32[]{:S(2)}, u32[]{:S(2)}) collective-permute-start(bf16[24,1024]{1,0:T(8,128)(2,1)S(1)} %collective-permute-done.22.refs_7_), channel_id=1, source_target_pairs={{0,1},{1,0},{2,3},{3,2},{4,5},{5,4},{6,7},{7,6},{8,9},{9,8},{10,11... | collective-permute-start | bytes 147464 | tf_op jit(solution)/shard_map/ppermute | solution.py:52
  53.2 1.2 %collective-permute-start.21 = (bf16[24,1024]{1,0:T(8,128)(2,1)S(1)}, bf16[24,1024]{1,0:T(8,128)(2,1)S(1)}, u32[]{:S(2)}, u32[]{:S(2)}) collective-permute-start(bf16[24,1024]{1,0:T(8,128)(2,1)S(1)} %collective-permute-done.20.refs_6_), channel_id=1, source_target_pairs={{0,1},{1,0},{2,3},{3,2},{4,5},{5,4},{6,7},{7,6},{8,9},{9,8},{10,11... | collective-permute-start | bytes 147464 | tf_op jit(solution)/shard_map/ppermute | solution.py:52
  53.3 1.3 %collective-permute-start.19 = (bf16[24,1024]{1,0:T(8,128)(2,1)S(1)}, bf16[24,1024]{1,0:T(8,128)(2,1)S(1)}, u32[]{:S(2)}, u32[]{:S(2)}) collective-permute-start(bf16[24,1024]{1,0:T(8,128)(2,1)S(1)} %collective-permute-done.18.refs_5_), channel_id=1, source_target_pairs={{0,1},{1,0},{2,3},{3,2},{4,5},{5,4},{6,7},{7,6},{8,9},{9,8},{10,11... | collective-permute-start | bytes 147464 | tf_op jit(solution)/shard_map/ppermute | solution.py:52
